TPU v7x, 32 devices: a whole 2x2x4 slice. The times are simulated.
32 devices in a mesh: fsdp: 2 (over x), ctx: 4 (over z), tp: 4 (over y, core).
Axes of the slice: x: 2, y: 2, z: 4, core: 2. Of those that a mesh axis runs over, the one named last changes fastest.
Arguments:
- hidden_in: bfloat16 [16384, 1792], P(('fsdp', 'ctx', 'tp')), may hold values from -6 to 6
- cotangent: bfloat16 [16384, 1792], P(('fsdp', 'ctx', 'tp')), may hold values from -6 to 6
- lengths: int32 [2, 4], replicated, may hold values from 1024 to 2048, as said below
- to_model: int32 [16384], P(('fsdp', 'ctx', 'tp')), may hold values from 0 to 16383, as said below
- to_loader: int32 [16384], P(('fsdp', 'ctx', 'tp')), may hold values from 0 to 16383, as said below
- conv_in: bfloat16 [1792, 2, 1792], P(('fsdp', 'ctx'), None, 'tp'), may hold values from -0.125 to 0.125
- conv_kernel: float32 [3, 1792], replicated, may hold values from -4.5 to 4.5
- conv_out: bfloat16 [1792, 1792], P('tp', ('fsdp', 'ctx')), may hold values from -0.375 to 0.375
- ffn_one_in: bfloat16 [1792, 2, 4864], P(('fsdp', 'ctx'), None, 'tp'), may hold values from -0.125 to 0.125
- ffn_one_out: bfloat16 [4864, 1792], P('tp', ('fsdp', 'ctx')), may hold values from -0.078125 to 0.078125
- attn_in: bfloat16 [1792, 16, 144], P(('fsdp', 'ctx'), 'tp'), may hold values from -0.125 to 0.125
- attn_out: bfloat16 [1792, 1792], P('tp', ('fsdp', 'ctx')), may hold values from -1 to 1
- ffn_two_in: bfloat16 [1792, 2, 4864], P(('fsdp', 'ctx'), None, 'tp'), may hold values from -0.125 to 0.125
- ffn_two_out: bfloat16 [4864, 1792], P('tp', ('fsdp', 'ctx')), may hold values from -0.078125 to 0.078125
- gains: float32 [4, 1792], replicated, may hold values from 0.5 to 1.5
Outputs:
- hidden_out: bfloat16 [16384, 1792], P(('fsdp', 'ctx', 'tp'))
- grad_in: bfloat16 [16384, 1792], P(('fsdp', 'ctx', 'tp'))
- grad_conv_in: float32 [1792, 2, 1792], P(('fsdp', 'ctx'), None, 'tp')
- grad_conv_kernel: float32 [3, 1792], replicated
- grad_conv_out: float32 [1792, 1792], P('tp', ('fsdp', 'ctx'))
- grad_ffn_one_in: float32 [1792, 2, 4864], P(('fsdp', 'ctx'), None, 'tp')
- grad_ffn_one_out: float32 [4864, 1792], P('tp', ('fsdp', 'ctx'))
- grad_attn_in: float32 [1792, 16, 144], P(('fsdp', 'ctx'), 'tp')
- grad_attn_out: float32 [1792, 1792], P('tp', ('fsdp', 'ctx'))
- grad_ffn_two_in: float32 [1792, 2, 4864], P(('fsdp', 'ctx'), None, 'tp')
- grad_ffn_two_out: float32 [4864, 1792], P('tp', ('fsdp', 'ctx'))
- grad_gains: float32 [4, 1792], replicated
Inputs may be any that keep to these rules, and one draw needn't show every extreme that they name: `lengths`: in each of the 2 rows one sequence, at a place drawn from the seed, has length exactly 2048. `to_model`: A permutation of the 16384 rows that keeps every row within its index of fsdp; every device receives exactly 32 rows from each device of its index of fsdp. `to_loader`: the inverse permutation of to_model.
All inputs are finite; a program needn't handle non-finite values.
Results may differ from a plain program's by a relative error of at most 0.015.
Values may be sent and summed in bfloat16 or wider, within the bound.
No kernel may reach another device: no remote copies, remote signals or barrier semaphores. Data moves between devices by JAX's collectives and lax.ppermute only.
A program may use at most 280 MiB of HBM per device.

v0:
```python
import jax
import jax.numpy as jnp
from jax import lax
from jax.sharding import PartitionSpec as P

F = 16
MAXLEN = 2048


epsilon = 1e-05
quad_scale = 0.7071067811865476


def from_behind(block, axis, distance):
    devices = range(lax.axis_size(axis))
    route = [(i - distance, i) for i in devices if i - distance in devices]
    return lax.ppermute(block, axis, route)


def prefix(part, axis, combine, identity, reverse):
    count = lax.axis_size(axis)
    place = lax.axis_index(axis)
    ahead = count - 1 - place if reverse else place
    gathered = lax.all_gather(part, axis)
    state = jnp.zeros_like(part) + jnp.asarray(identity, part.dtype)

    def one(lap, state):
        source = count - 1 - lap if reverse else lap
        return combine(state, lax.dynamic_index_in_dim(gathered, source, 0, False))

    return lax.fori_loop(0, ahead, one, state)


def features(vector):
    quad = (vector[..., :, None] * vector[..., None, :]).reshape(
        vector.shape[:-1] + (vector.shape[-1] * vector.shape[-1],)
    ) * quad_scale
    return jnp.concatenate([quad, vector, jnp.ones(vector.shape[:-1] + (1,), jnp.float32)], axis=-1)


def norm_rows(stream, gain):
    return stream * lax.rsqrt(jnp.mean(stream * stream, axis=-1, keepdims=True) + epsilon) * gain


def swiglu(projected_features):
    return jax.nn.silu(projected_features[:, 0]) * projected_features[:, 1]


def slot_index(peer, order_key, per_peer):
    same = peer[:, None] == peer[None, :]
    before = order_key[None, :] < order_key[:, None]
    return peer * per_peer + jnp.sum((same & before).astype(jnp.int32), axis=1)


def regroup(first, second, order, position):
    received = (
        lax.all_to_all(first[order], ("ctx", "tp"), split_axis=0, concat_axis=0, tiled=True),
        lax.all_to_all(second[order], ("ctx", "tp"), split_axis=0, concat_axis=0, tiled=True),
    )
    return (received[0][position], received[1][position])


def spread(row_block):
    return lax.all_gather(row_block, "tp", axis=0, tiled=True)


def collect(partial_value):
    return lax.psum_scatter(partial_value, "tp", scatter_dimension=0, tiled=True)


def fetch_layer(first_in, first_out, second_in, second_out):
    return (
        lax.all_gather(first_in, ("fsdp", "ctx"), axis=0, tiled=True),
        lax.all_gather(first_out, ("fsdp", "ctx"), axis=1, tiled=True),
        lax.all_gather(second_in, ("fsdp", "ctx"), axis=0, tiled=True),
        lax.all_gather(second_out, ("fsdp", "ctx"), axis=1, tiled=True),
    )


def reduce_layer(first_in, first_out, second_in, second_out):
    return (
        lax.psum_scatter(first_in, ("fsdp", "ctx"), scatter_dimension=0, tiled=True),
        lax.psum_scatter(first_out, ("fsdp", "ctx"), scatter_dimension=1, tiled=True),
        lax.psum_scatter(second_in, ("fsdp", "ctx"), scatter_dimension=0, tiled=True),
        lax.psum_scatter(second_out, ("fsdp", "ctx"), scatter_dimension=1, tiled=True),
    )


def conv_forward(rms_normalized_input, input_weight, output_weight, kernel, seq_count, slot_rows):
    projected_features = jnp.einsum(
        "rd,dgc->rgc", rms_normalized_input, input_weight, preferred_element_type=jnp.float32
    )
    signal = projected_features[:, 0].astype(jnp.bfloat16).reshape(seq_count, slot_rows, -1)
    gate_value = projected_features[:, 1].reshape(seq_count, slot_rows, -1)
    before = from_behind(signal[:, slot_rows - 2 :], "ctx", 1)
    widened = jnp.concatenate([before, signal], axis=1).astype(jnp.float32)
    tap_rows = (widened[:, 2:], widened[:, 1:-1], widened[:, :-2])
    mixture = kernel[0] * tap_rows[0] + kernel[1] * tap_rows[1] + kernel[2] * tap_rows[2]
    hidden_activation = (
        (mixture * gate_value).astype(jnp.bfloat16).reshape(seq_count * slot_rows, -1)
    )
    partial_value = jnp.dot(hidden_activation, output_weight, preferred_element_type=jnp.float32)
    return (partial_value, (tap_rows, gate_value, mixture, hidden_activation))


def conv_backward(
    rms_normalized_input,
    grad_out,
    input_weight,
    output_weight,
    kernel,
    stored,
    seq_count,
    slot_rows,
):
    tap_rows, gate_value, mixture, hidden_activation = stored
    grad_hidden = jnp.einsum(
        "rd,cd->rc", grad_out, output_weight, preferred_element_type=jnp.float32
    ).reshape(seq_count, slot_rows, -1)
    grad_w_out = jnp.einsum(
        "rc,rd->cd", hidden_activation, grad_out, preferred_element_type=jnp.float32
    )
    grad_mix = grad_hidden * gate_value
    grad_gate = grad_hidden * mixture
    after = from_behind(grad_mix[:, :2], "ctx", -1)
    widened = jnp.concatenate([grad_mix, after], axis=1)
    grad_signal = kernel[0] * grad_mix + kernel[1] * widened[:, 1:-1] + kernel[2] * widened[:, 2:]
    grad_kernel = jnp.stack([jnp.sum(grad_mix * tap, axis=(0, 1)) for tap in tap_rows])
    grad_proj = (
        jnp.stack([grad_signal, grad_gate], axis=2)
        .astype(jnp.bfloat16)
        .reshape(seq_count * slot_rows, 2, -1)
    )
    grad_w_in = jnp.einsum(
        "rd,rgc->dgc", rms_normalized_input, grad_proj, preferred_element_type=jnp.float32
    )
    grad_normed = jnp.einsum(
        "rgc,dgc->rd", grad_proj, input_weight, preferred_element_type=jnp.float32
    )
    return (grad_normed, grad_w_in, grad_w_out, grad_kernel)


def ffn_forward(rms_normalized_input, input_weight, output_weight):
    projected_features = jnp.einsum(
        "rd,dgf->rgf", rms_normalized_input, input_weight, preferred_element_type=jnp.float32
    )
    hidden_activation = swiglu(projected_features).astype(jnp.bfloat16)
    partial_value = jnp.dot(hidden_activation, output_weight, preferred_element_type=jnp.float32)
    return (partial_value, (projected_features, hidden_activation))


def ffn_backward(rms_normalized_input, grad_out, input_weight, output_weight, stored):
    projected_features, hidden_activation = stored
    grad_hidden = jnp.einsum(
        "rd,fd->rf", grad_out, output_weight, preferred_element_type=jnp.float32
    )
    grad_w_out = jnp.einsum(
        "rf,rd->fd", hidden_activation, grad_out, preferred_element_type=jnp.float32
    )
    unused, pull = jax.vjp(swiglu, projected_features)
    grad_proj = pull(grad_hidden)[0].astype(jnp.bfloat16)
    grad_w_in = jnp.einsum(
        "rd,rgf->dgf", rms_normalized_input, grad_proj, preferred_element_type=jnp.float32
    )
    grad_normed = jnp.einsum(
        "rgf,dgf->rd", grad_proj, input_weight, preferred_element_type=jnp.float32
    )
    return (grad_normed, grad_w_in, grad_w_out)


def causal_mask(slot_rows):
    return jnp.arange(slot_rows)[:, None] >= jnp.arange(slot_rows)[None, :]


def attn_forward(rms_normalized_input, input_weight, output_weight, seq_count, slot_rows):
    projected_features = jnp.einsum(
        "rd,dhe->rhe", rms_normalized_input, input_weight, preferred_element_type=jnp.float32
    )
    projected_features = projected_features.reshape(seq_count, slot_rows, input_weight.shape[1], -1)
    queries = (0.5 * projected_features[..., :F]).astype(jnp.bfloat16)
    key_rows = (0.5 * projected_features[..., F : 2 * F]).astype(jnp.bfloat16)
    values = projected_features[..., 2 * F :].astype(jnp.bfloat16)
    extended = jnp.concatenate([values, jnp.ones(values.shape[:-1] + (1,), jnp.bfloat16)], axis=-1)
    scores = jnp.einsum("sphf,sqhf->shpq", queries, key_rows, preferred_element_type=jnp.float32)
    weight = jnp.where(causal_mask(slot_rows), 1.0 + scores + 0.5 * scores * scores, 0.0).astype(
        jnp.bfloat16
    )
    q_feat = features(queries.astype(jnp.float32)).astype(jnp.bfloat16)
    k_feat = features(key_rows.astype(jnp.float32)).astype(jnp.bfloat16)
    states = jnp.einsum("sqhe,sqhv->shev", k_feat, extended, preferred_element_type=jnp.float32)
    earlier = prefix(states, "ctx", jnp.add, jnp.zeros_like(states), False).astype(jnp.bfloat16)
    totals = jnp.einsum(
        "shpq,sqhv->sphv", weight, extended, preferred_element_type=jnp.float32
    ) + jnp.einsum("sphe,shev->sphv", q_feat, earlier, preferred_element_type=jnp.float32)
    per_head_output = (
        (totals[..., :-1] / totals[..., -1:])
        .astype(jnp.bfloat16)
        .reshape(seq_count * slot_rows, -1)
    )
    partial_value = jnp.dot(per_head_output, output_weight, preferred_element_type=jnp.float32)
    return (
        partial_value,
        (
            queries,
            key_rows,
            extended,
            scores,
            weight,
            q_feat,
            k_feat,
            earlier,
            totals,
            per_head_output,
        ),
    )


def attn_backward(
    rms_normalized_input, grad_out, input_weight, output_weight, stored, seq_count, slot_rows
):
    (
        queries,
        key_rows,
        extended,
        scores,
        weight,
        q_feat,
        k_feat,
        earlier,
        totals,
        per_head_output,
    ) = stored
    grad_heads = jnp.einsum(
        "rd,cd->rc", grad_out, output_weight, preferred_element_type=jnp.float32
    )
    grad_heads = grad_heads.reshape(seq_count, slot_rows, input_weight.shape[1], -1)
    grad_w_out = jnp.einsum(
        "rc,rd->cd", per_head_output, grad_out, preferred_element_type=jnp.float32
    )
    denominator = totals[..., -1:]
    grad_num = grad_heads / denominator
    grad_den = -jnp.sum(grad_heads * totals[..., :-1], axis=-1, keepdims=True) / (
        denominator * denominator
    )
    grad_total = jnp.concatenate([grad_num, grad_den], axis=-1).astype(jnp.bfloat16)
    grad_weight = jnp.einsum(
        "sphv,sqhv->shpq", grad_total, extended, preferred_element_type=jnp.float32
    )
    grad_qf = jnp.einsum("sphv,shev->sphe", grad_total, earlier, preferred_element_type=jnp.float32)
    grad_prior = jnp.einsum(
        "sphe,sphv->shev", q_feat, grad_total, preferred_element_type=jnp.float32
    )
    grad_state = prefix(grad_prior, "ctx", jnp.add, jnp.zeros_like(grad_prior), True).astype(
        jnp.bfloat16
    )
    grad_ext = jnp.einsum(
        "shpq,sphv->sqhv", weight, grad_total, preferred_element_type=jnp.float32
    ) + jnp.einsum("sqhe,shev->sqhv", k_feat, grad_state, preferred_element_type=jnp.float32)
    grad_kf = jnp.einsum(
        "sqhv,shev->sqhe", extended, grad_state, preferred_element_type=jnp.float32
    )
    grad_score = jnp.where(causal_mask(slot_rows), grad_weight * (1.0 + scores), 0.0).astype(
        jnp.bfloat16
    )
    unused, pull_query = jax.vjp(features, queries.astype(jnp.float32))
    unused, pull_key = jax.vjp(features, key_rows.astype(jnp.float32))
    grad_query = (
        jnp.einsum("shpq,sqhf->sphf", grad_score, key_rows, preferred_element_type=jnp.float32)
        + pull_query(grad_qf)[0]
    )
    grad_key = (
        jnp.einsum("shpq,sphf->sqhf", grad_score, queries, preferred_element_type=jnp.float32)
        + pull_key(grad_kf)[0]
    )
    grad_proj = jnp.concatenate(
        [0.5 * grad_query, 0.5 * grad_key, grad_ext[..., :-1]], axis=-1
    ).astype(jnp.bfloat16)
    grad_proj = grad_proj.reshape(seq_count * slot_rows, input_weight.shape[1], -1)
    grad_w_in = jnp.einsum(
        "rd,rhe->dhe", rms_normalized_input, grad_proj, preferred_element_type=jnp.float32
    )
    grad_normed = jnp.einsum(
        "rhe,dhe->rd", grad_proj, input_weight, preferred_element_type=jnp.float32
    )
    return (grad_normed, grad_w_in, grad_w_out)


def norm_back(stream, grad_normed, gain):
    unused, pull = jax.vjp(norm_rows, stream, gain)
    return pull(grad_normed)


def shards(
    hidden_in,
    cotangent,
    lengths,
    to_model,
    to_loader,
    conv_in,
    conv_kernel,
    conv_out,
    ffn_one_in,
    ffn_one_out,
    attn_in,
    attn_out,
    ffn_two_in,
    ffn_two_out,
    gains,
):
    tp_size = lax.axis_size("tp")
    ctx_size = lax.axis_size("ctx")
    group_size = ctx_size * tp_size
    row_count = hidden_in.shape[0]
    per_peer = row_count // group_size
    slot_rows = MAXLEN // ctx_size
    block_rows = row_count * tp_size
    seq_count = block_rows // slot_rows
    tp_rank = lax.axis_index("tp")
    counter = jnp.arange(row_count, dtype=jnp.int32)
    send_slot = slot_index(to_loader // row_count % group_size, counter, per_peer)
    recv_slot = slot_index(to_model // row_count % group_size, to_model % row_count, per_peer)
    stream_in, cotan_rows = regroup(hidden_in, cotangent, jnp.argsort(send_slot), recv_slot)
    seq_lengths = lax.dynamic_index_in_dim(lengths, lax.axis_index("fsdp"), 0, keepdims=False)
    position = lax.axis_index("ctx") * slot_rows + jnp.arange(slot_rows, dtype=jnp.int32)
    valid_block = (position[None, :] < seq_lengths[:, None]).astype(jnp.float32).reshape(block_rows)
    valid_rows = lax.dynamic_slice_in_dim(valid_block, tp_rank * row_count, row_count)[:, None]
    channels = conv_in.shape[2]
    kernel = lax.dynamic_slice_in_dim(conv_kernel, tp_rank * channels, channels, 1)
    stream_zero = stream_in.astype(jnp.float32)
    layer_one = fetch_layer(conv_in, conv_out, ffn_one_in, ffn_one_out)
    normed_zero = spread(norm_rows(stream_zero, gains[0]).astype(jnp.bfloat16))
    partial_value, stored_zero = conv_forward(
        normed_zero, layer_one[0], layer_one[1], kernel, seq_count, slot_rows
    )
    stream_one = stream_zero + valid_rows * collect(partial_value)
    normed_one = spread(norm_rows(stream_one, gains[1]).astype(jnp.bfloat16))
    partial_value, stored_one = ffn_forward(normed_one, layer_one[2], layer_one[3])
    stream_two = stream_one + valid_rows * collect(partial_value)
    layer_two = fetch_layer(attn_in, attn_out, ffn_two_in, ffn_two_out)
    normed_two = spread(norm_rows(stream_two, gains[2]).astype(jnp.bfloat16))
    partial_value, stored_two = attn_forward(
        normed_two, layer_two[0], layer_two[1], seq_count, slot_rows
    )
    stream_three = stream_two + valid_rows * collect(partial_value)
    normed_three = spread(norm_rows(stream_three, gains[3]).astype(jnp.bfloat16))
    partial_value, stored_three = ffn_forward(normed_three, layer_two[2], layer_two[3])
    stream_four = stream_three + valid_rows * collect(partial_value)
    own_streams = (stream_zero, stream_one, stream_two, stream_three)
    upstream = cotan_rows.astype(jnp.float32)

    def back_step(carry, index, backward_fn):
        grad_out = spread((valid_rows * carry).astype(jnp.bfloat16))
        results = backward_fn(grad_out)
        grad_stream, gain_grad = norm_back(own_streams[index], collect(results[0]), gains[index])
        return (carry + grad_stream, gain_grad, results[1:])

    layer_two = fetch_layer(attn_in, attn_out, ffn_two_in, ffn_two_out)
    upstream, gain_three, found = back_step(
        upstream,
        3,
        lambda grad_out: ffn_backward(
            normed_three, grad_out, layer_two[2], layer_two[3], stored_three
        ),
    )
    grad_f2_in, grad_f2_out = found
    upstream, gain_two, found = back_step(
        upstream,
        2,
        lambda grad_out: attn_backward(
            normed_two, grad_out, layer_two[0], layer_two[1], stored_two, seq_count, slot_rows
        ),
    )
    grad_a_in, grad_a_out = found
    summed_two = reduce_layer(grad_a_in, grad_a_out, grad_f2_in, grad_f2_out)
    layer_one = fetch_layer(conv_in, conv_out, ffn_one_in, ffn_one_out)
    upstream, gain_one, found = back_step(
        upstream,
        1,
        lambda grad_out: ffn_backward(normed_one, grad_out, layer_one[2], layer_one[3], stored_one),
    )
    grad_f1_in, grad_f1_out = found
    upstream, gain_zero, found = back_step(
        upstream,
        0,
        lambda grad_out: conv_backward(
            normed_zero,
            grad_out,
            layer_one[0],
            layer_one[1],
            kernel,
            stored_zero,
            seq_count,
            slot_rows,
        ),
    )
    grad_c_in, grad_c_out, grad_kernel = found
    summed_one = reduce_layer(grad_c_in, grad_c_out, grad_f1_in, grad_f1_out)
    kernel_full = jnp.zeros(conv_kernel.shape, jnp.float32)
    kernel_full = lax.dynamic_update_slice_in_dim(kernel_full, grad_kernel, tp_rank * channels, 1)
    gain_stack = jnp.stack([gain_zero, gain_one, gain_two, gain_three])
    gain_total, kernel_total = lax.psum((gain_stack, kernel_full), ("fsdp", "ctx", "tp"))
    hidden_out, grad_in = regroup(
        stream_four.astype(jnp.bfloat16),
        upstream.astype(jnp.bfloat16),
        jnp.argsort(recv_slot),
        send_slot,
    )
    return (
        hidden_out,
        grad_in,
        summed_one[0],
        kernel_total,
        summed_one[1],
        summed_one[2],
        summed_one[3],
        summed_two[0],
        summed_two[1],
        summed_two[2],
        summed_two[3],
        gain_total,
    )


def solution(mesh):
    return jax.shard_map(
        shards,
        mesh=mesh,
        in_specs=(
            P(("fsdp", "ctx", "tp"), None),
            P(("fsdp", "ctx", "tp"), None),
            P(),
            P(("fsdp", "ctx", "tp")),
            P(("fsdp", "ctx", "tp")),
            P(("fsdp", "ctx"), None, "tp"),
            P(),
            P("tp", ("fsdp", "ctx")),
            P(("fsdp", "ctx"), None, "tp"),
            P("tp", ("fsdp", "ctx")),
            P(("fsdp", "ctx"), "tp", None),
            P("tp", ("fsdp", "ctx")),
            P(("fsdp", "ctx"), None, "tp"),
            P("tp", ("fsdp", "ctx")),
            P(),
        ),
        out_specs=(
            P(("fsdp", "ctx", "tp"), None),
            P(("fsdp", "ctx", "tp"), None),
            P(("fsdp", "ctx"), None, "tp"),
            P(),
            P("tp", ("fsdp", "ctx")),
            P(("fsdp", "ctx"), None, "tp"),
            P("tp", ("fsdp", "ctx")),
            P(("fsdp", "ctx"), "tp", None),
            P("tp", ("fsdp", "ctx")),
            P(("fsdp", "ctx"), None, "tp"),
            P("tp", ("fsdp", "ctx")),
            P(),
        ),
        check_vma=False,
    )
```

profile of v0, /device:TPU:0, one launch (start us, length us, event | category | flops | bytes accessed | tf_op | source)
XLA Modules:
  0.0 4131.8 jit_solution(15563865725609516576)
XLA Ops:
  26.3 61.1 %all-to-all-done = bf16[16,32,1792]{2,1,0:T(8,128)(2,1)S(1)} async-done(((bf16[16,32,1792]{2,1,0:T(8,128)(2,1)}), bf16[16,32,1792]{2,1,0:T(8,128)(2,1)S(1)}, u32[]{:S(2)}, u32[]{:S(2)}) %all-to-all-start) | async-done | bytes 1835040 | tf_op jit(solution)/shard_map/all_to_all | solution.py:57
  109.1 57.3 %all-gather.21.cloned.1.call-done = bf16[2048,1792]{1,0:T(8,128)(2,1)} async-done(((bf16[512,1792]{1,0:T(8,128)(2,1)}), bf16[2048,1792]{1,0:T(8,128)(2,1)}) %all-gather.21.cloned.1.call-update) | async-done | bytes 7340048 | tf_op jit(solution)/shard_map/all_gather | solution.py:64
  230.2 109.5 %reduce-scatter.23.cloned.1.call-done = f32[512,1792]{1,0:T(8,128)} async-done(((f32[2048,1792]{1,0:T(8,128)}), f32[512,1792]{1,0:T(8,128)}) %reduce-scatter.23.cloned.1.call-update) | async-done | bytes 3670032 | tf_op jit(solution)/shard_map/reduce_scatter | solution.py:68
  347.1 130.1 %all-gather.29.cloned.1.call-done = bf16[1792,2,1216]{2,0,1:T(8,128)(2,1)} async-done(((bf16[224,2,1216]{2,0,1:T(8,128)(2,1)}), bf16[1792,2,1216]{2,0,1:T(8,128)(2,1)}) %all-gather.29.cloned.1.call-update) | async-done | bytes 8716304 | tf_op jit(solution)/shard_map/all_gather | solution.py:75
  477.2 52.5 %all-gather.27.cloned.1.call-done = bf16[2048,1792]{1,0:T(8,128)(2,1)} async-done(((bf16[512,1792]{1,0:T(8,128)(2,1)}), bf16[2048,1792]{1,0:T(8,128)(2,1)}) %all-gather.27.cloned.1.call-update) | async-done | bytes 7340048 | tf_op jit(solution)/shard_map/all_gather | solution.py:64
  674.6 68.3 %reduce-scatter.25.cloned.1.call-done = f32[512,1792]{1,0:T(8,128)} async-done(((f32[2048,1792]{1,0:T(8,128)}), f32[512,1792]{1,0:T(8,128)}) %reduce-scatter.25.cloned.1.call-update) | async-done | bytes 3670032 | tf_op jit(solution)/shard_map/reduce_scatter | solution.py:68
  752.6 61.0 %all-gather.35.cloned.1.call-done = bf16[1792,4,144]{2,1,0:T(4,128)(2,1)} async-done(((bf16[224,4,144]{2,1,0:T(4,128)(2,1)}), bf16[1792,4,144]{2,1,0:T(4,128)(2,1)}) %all-gather.35.cloned.1.call-update) | async-done | bytes 2064400 | tf_op jit(solution)/shard_map/all_gather | solution.py:73
  908.2 144.6 %all-gather.53.cloned.1.call-done = f32[16,4,273,113]{3,1,2,0:T(4,128)} async-done(((f32[4,4,273,113]{3,1,2,0:T(4,128)}), f32[16,4,273,113]{3,1,2,0:T(4,128)}) %all-gather.53.cloned.1.call-update) | async-done | bytes 7897360 | tf_op jit(solution)/shard_map/all_gather | solution.py:24
  1113.6 109.7 %reduce-scatter.27.cloned.1.call-done = f32[512,1792]{1,0:T(8,128)} async-done(((f32[2048,1792]{1,0:T(8,128)}), f32[512,1792]{1,0:T(8,128)}) %reduce-scatter.27.cloned.1.call-update) | async-done | bytes 3670032 | tf_op jit(solution)/shard_map/reduce_scatter | solution.py:68
  1232.4 128.4 %all-gather.41.cloned.1.call-done = bf16[1792,2,1216]{2,0,1:T(8,128)(2,1)} async-done(((bf16[224,2,1216]{2,0,1:T(8,128)(2,1)}), bf16[1792,2,1216]{2,0,1:T(8,128)(2,1)}) %all-gather.41.cloned.1.call-update) | async-done | bytes 8716304 | tf_op jit(solution)/shard_map/all_gather | solution.py:75
  1438.4 54.6 %all-gather.43.cloned.1.call-done = bf16[1216,1792]{0,1:T(8,128)(2,1)} async-done(((bf16[1216,224]{0,1:T(8,128)(2,1)}), bf16[1216,1792]{0,1:T(8,128)(2,1)}) %all-gather.43.cloned.1.call-update) | async-done | bytes 4358160 | tf_op jit(solution)/shard_map/all_gather | solution.py:76
  1597.4 113.0 %reduce-scatter.31.cloned.1.call-done = f32[512,1792]{1,0:T(8,128)} async-done(((f32[2048,1792]{1,0:T(8,128)}), f32[512,1792]{1,0:T(8,128)}) %reduce-scatter.31.cloned.1.call-update) | async-done | bytes 3670032 | tf_op jit(solution)/shard_map/reduce_scatter | solution.py:68
  1827.4 126.5 %all-gather.55.cloned.1.call-done = f32[16,4,273,113]{3,1,2,0:T(4,128)} async-done(((f32[4,4,273,113]{3,1,2,0:T(4,128)}), f32[16,4,273,113]{3,1,2,0:T(4,128)}) %all-gather.55.cloned.1.call-update) | async-done | bytes 7897360 | tf_op jit(solution)/shard_map/all_gather | solution.py:24
  2029.9 93.4 %reduce-scatter.33.cloned.1.call-done = f32[512,1792]{1,0:T(8,128)} async-done(((f32[2048,1792]{1,0:T(8,128)}), f32[512,1792]{1,0:T(8,128)}) %reduce-scatter.33.cloned.1.call-update) | async-done | bytes 3670032 | tf_op jit(solution)/shard_map/reduce_scatter | solution.py:68
  2128.0 110.9 %reduce-scatter.29.cloned.1.call-done = f32[512,1792]{1,0:T(8,128)} async-done(((f32[2048,1792]{1,0:T(8,128)}), f32[512,1792]{1,0:T(8,128)}) %reduce-scatter.29.cloned.1.call-update) | async-done | bytes 3670032 | tf_op jit(solution)/shard_map/reduce_scatter | solution.py:68
  2352.6 113.0 %reduce-scatter.35.cloned.1.call-done = f32[512,1792]{1,0:T(8,128)} async-done(((f32[2048,1792]{1,0:T(8,128)}), f32[512,1792]{1,0:T(8,128)}) %reduce-scatter.35.cloned.1.call-update) | async-done | bytes 3670032 | tf_op jit(solution)/shard_map/reduce_scatter | solution.py:68
  2820.6 265.8 %reduce-scatter.45.cloned.1.call-done = f32[224,2,1216]{2,0,1:T(8,128)} async-done(((f32[1792,2,1216]{2,0,1:T(8,128)}), f32[224,2,1216]{2,0,1:T(8,128)}) %reduce-scatter.45.cloned.1.call-update) | async-done | bytes 2179088 | tf_op jit(solution)/shard_map/reduce_scatter | solution.py:84
  3091.1 79.4 %reduce-scatter.53.cloned.1.call-done = f32[224,448]{1,0:T(8,128)} async-done(((f32[1792,448]{1,0:T(8,128)}), f32[224,448]{1,0:T(8,128)}) %reduce-scatter.53.cloned.1.call-update) | async-done | bytes 401424
  3172.4 95.3 %reduce-scatter.51.cloned.1.call-done = f32[224,576]{1,0:T(8,128)} async-done(((f32[1792,576]{1,0:T(8,128)}), f32[224,576]{1,0:T(8,128)}) %reduce-scatter.51.cloned.1.call-update) | async-done | bytes 516112
  3273.0 304.5 %reduce-scatter.41.cloned.1.call-done = f32[224,2,1216]{2,0,1:T(8,128)} async-done(((f32[1792,2,1216]{2,0,1:T(8,128)}), f32[224,2,1216]{2,0,1:T(8,128)}) %reduce-scatter.41.cloned.1.call-update) | async-done | bytes 2179088 | tf_op jit(solution)/shard_map/reduce_scatter | solution.py:84
  3582.6 78.6 %reduce-scatter.49.cloned.1.call-done = f32[224,448]{1,0:T(8,128)} async-done(((f32[1792,448]{1,0:T(8,128)}), f32[224,448]{1,0:T(8,128)}) %reduce-scatter.49.cloned.1.call-update) | async-done | bytes 401424
  3663.2 134.0 %reduce-scatter.39.cloned.1.call-done = f32[224,2,448]{2,0,1:T(8,128)} async-done(((f32[1792,2,448]{2,0,1:T(8,128)}), f32[224,2,448]{2,0,1:T(8,128)}) %reduce-scatter.39.cloned.1.call-update) | async-done | bytes 802832 | tf_op jit(solution)/shard_map/reduce_scatter | solution.py:82
  3850.9 110.2 %reduce-scatter.47.cloned.1.call-done = f32[1216,224]{0,1:T(8,128)} async-done(((f32[1216,1792]{0,1:T(8,128)}), f32[1216,224]{0,1:T(8,128)}) %reduce-scatter.47.cloned.1.call-update) | async-done | bytes 1089552 | tf_op jit(solution)/shard_map/reduce_scatter | solution.py:85
  3961.0 163.5 %reduce-scatter.43.cloned.1.call-done = f32[1216,224]{0,1:T(8,128)} async-done(((f32[1216,1792]{0,1:T(8,128)}), f32[1216,224]{0,1:T(8,128)}) %reduce-scatter.43.cloned.1.call-update) | async-done | bytes 1089552 | tf_op jit(solution)/shard_map/reduce_scatter | solution.py:85
  (451 shorter events, 1365.6 us)
Async XLA Ops:
  96.7 243.0 %reduce-scatter.23.cloned.1.call-start = ((), (), s32[]{:S(2)}) async-start(), calls=%async_computation.23 | async-start | bytes 18350080 | tf_op jit(solution)/shard_map/reduce_scatter | solution.py:68
  227.6 249.6 %all-gather.29.cloned.1.call-start = ((), (), s32[]{:S(2)}) async-start(), calls=%async_computation.25 | async-start | bytes 10321920 | tf_op jit(solution)/shard_map/all_gather | solution.py:75
  229.9 299.8 %all-gather.27.cloned.1.call-start = ((), (), s32[]{:S(2)}) async-start(), calls=%async_computation.24 | async-start | bytes 9175040 | tf_op jit(solution)/shard_map/all_gather | solution.py:64
  345.9 264.2 %all-gather.31.cloned.1.call-start = ((), (), s32[]{:S(2)}) async-start(), calls=%async_computation.26 | async-start | bytes 5160960 | tf_op jit(solution)/shard_map/all_gather | solution.py:76
  346.7 396.3 %reduce-scatter.25.cloned.1.call-start = ((), (), s32[]{:S(2)}) async-start(), calls=%async_computation.27 | async-start | bytes 18350080 | tf_op jit(solution)/shard_map/reduce_scatter | solution.py:68
  752.5 300.4 %all-gather.53.cloned.1.call-start = ((), (), s32[]{:S(2)}) async-start(), calls=%async_computation.49 | async-start | bytes 11182080 | tf_op jit(solution)/shard_map/all_gather | solution.py:24
  894.9 328.4 %reduce-scatter.27.cloned.1.call-start = ((), (), s32[]{:S(2)}) async-start(), calls=%async_computation.31 | async-start | bytes 18350080 | tf_op jit(solution)/shard_map/reduce_scatter | solution.py:68
  1111.2 249.6 %all-gather.41.cloned.1.call-start = ((), (), s32[]{:S(2)}) async-start(), calls=%async_computation.33 | async-start | bytes 10321920 | tf_op jit(solution)/shard_map/all_gather | solution.py:75
  1113.6 299.2 %all-gather.39.cloned.1.call-start = ((), (), s32[]{:S(2)}) async-start(), calls=%async_computation.32 | async-start | bytes 9175040 | tf_op jit(solution)/shard_map/all_gather | solution.py:64
  1230.7 262.3 %all-gather.43.cloned.1.call-start = ((), (), s32[]{:S(2)}) async-start(), calls=%async_computation.34 | async-start | bytes 5160960 | tf_op jit(solution)/shard_map/all_gather | solution.py:76
  1231.3 313.6 %all-gather.45.cloned.1.call-start = ((), (), s32[]{:S(2)}) async-start(), calls=%async_computation.36 | async-start | bytes 9175040 | tf_op jit(solution)/shard_map/all_gather | solution.py:64
  1231.9 478.5 %reduce-scatter.31.cloned.1.call-start = ((), (), s32[]{:S(2)}) async-start(), calls=%async_computation.37 | async-start | bytes 18350080 | tf_op jit(solution)/shard_map/reduce_scatter | solution.py:68
  1795.0 328.3 %reduce-scatter.33.cloned.1.call-start = ((), (), s32[]{:S(2)}) async-start(), calls=%async_computation.39 | async-start | bytes 18350080 | tf_op jit(solution)/shard_map/reduce_scatter | solution.py:68
  2029.9 272.0 %all-gather.49.cloned.1.call-start = ((), (), s32[]{:S(2)}) async-start(), calls=%async_computation.40 | async-start | bytes 9175040 | tf_op jit(solution)/shard_map/all_gather | solution.py:64
  2476.5 252.6 %reduce-scatter.37.cloned.1.call-start = ((), (), s32[]{:S(2)}) async-start(), calls=%async_computation.43 | async-start | bytes 18350080 | tf_op jit(solution)/shard_map/reduce_scatter | solution.py:68
  2584.1 502.2 %reduce-scatter.45.cloned.1.call-start = ((), (), s32[]{:S(2)}) async-start(), calls=%async_computation.47 | async-start | bytes 20643840 | tf_op jit(solution)/shard_map/reduce_scatter | solution.py:84
  2611.4 559.1 %reduce-scatter.53.cloned.1.call-start = ((), (), s32[]{:S(2)}) async-start(), calls=%async_computation.53 | async-start | bytes 4128768
  2622.0 645.7 %reduce-scatter.51.cloned.1.call-start = ((), (), s32[]{:S(2)}) async-start(), calls=%async_computation.52 | async-start | bytes 5160960
  2632.4 945.1 %reduce-scatter.41.cloned.1.call-start = ((), (), s32[]{:S(2)}) async-start(), calls=%async_computation.45 | async-start | bytes 20643840 | tf_op jit(solution)/shard_map/reduce_scatter | solution.py:84
  2659.4 1001.8 %reduce-scatter.49.cloned.1.call-start = ((), (), s32[]{:S(2)}) async-start(), calls=%async_computation.51 | async-start | bytes 4128768
  2669.8 1127.3 %reduce-scatter.39.cloned.1.call-start = ((), (), s32[]{:S(2)}) async-start(), calls=%async_computation.44 | async-start | bytes 8257536 | tf_op jit(solution)/shard_map/reduce_scatter | solution.py:82
  2683.1 1278.0 %reduce-scatter.47.cloned.1.call-start = ((), (), s32[]{:S(2)}) async-start(), calls=%async_computation.48 | async-start | bytes 10321920 | tf_op jit(solution)/shard_map/reduce_scatter | solution.py:85
  2698.7 1425.8 %reduce-scatter.43.cloned.1.call-start = ((), (), s32[]{:S(2)}) async-start(), calls=%async_computation.46 | async-start | bytes 10321920 | tf_op jit(solution)/shard_map/reduce_scatter | solution.py:85
  2794.3 1050.0 %all-to-all-start.3 = ((bf16[16,32,1792]{2,1,0:T(8,128)(2,1)}), bf16[16,32,1792]{2,1,0:T(8,128)(2,1)}, u32[]{:S(2)}, u32[]{:S(2)}) async-start(bf16[16,32,1792]{2,1,0:T(8,128)(2,1)} %bitcast.241), calls=%async_computation.11 | async-start | bytes 3670016 | tf_op jit(solution)/shard_map/all_to_all | solution.py:58
  (109 other events, 7394.7 us)
Sparse Core Ops, SparseCore 0:
  10.1 98.9 all-gather.22
  227.7 111.9 reduce-scatter.22
  342.3 134.8 all-gather.28
  531.8 78.2 all-gather.30
  626.4 116.4 reduce-scatter.24
  745.6 67.9 all-gather.34
  894.1 158.7 all-gather.52
  1111.3 111.9 reduce-scatter.26
  1225.9 134.8 all-gather.40
  1414.7 78.2 all-gather.42
  1597.5 112.9 reduce-scatter.30
  1795.2 158.7 all-gather.54
  2012.2 111.0 reduce-scatter.32
  2125.9 112.9 reduce-scatter.28
  2352.6 112.9 reduce-scatter.34
  2584.2 114.1 reduce-scatter.36
  2702.2 384.0 reduce-scatter.44
  3090.4 80.0 reduce-scatter.52
  3174.5 93.1 reduce-scatter.50
  3272.0 305.4 reduce-scatter.40
  3581.1 80.0 reduce-scatter.48
  3664.8 132.3 reduce-scatter.38
  3801.2 159.7 reduce-scatter.46
  3965.7 158.7 reduce-scatter.42
  (10 shorter events, 505.3 us)
where the time goes:
time: 4140 us; the launch traced here: 4130 us
  waiting for transfers between devices  3260 us (79%)
  matrix products  459 us (11%)
  local copies, waits for them, and re-layouts  159 us (4%)
  other arithmetic  144 us (3%)
  starting transfers between devices  51.9 us (1%)
  blocking collectives  44.2 us (1%)
    reduce_scatter x8, waiting for transfers between devices, collect(): lax.psum_scatter(partial_value, 'tp', scatter_dimension=0, tiled=True)  718 us
    reduce_scatter x2, waiting for transfers between devices, reduce_layer(): lax.psum_scatter(second_in, ('fsdp', 'ctx'), scatter_dimension=0, tiled=T...  570 us
    all_gather x8, waiting for transfers between devices, spread(): return lax.all_gather(row_block, 'tp', axis=0, tiled=True)  417 us
    reduce_scatter x2, waiting for transfers between devices, reduce_layer(): lax.psum_scatter(second_out, ('fsdp', 'ctx'), scatter_dimension=1, tiled=...  274 us
    all_gather x2, waiting for transfers between devices, prefix(): gathered = lax.all_gather(part, axis)  271 us
    all_gather x2, waiting for transfers between devices, fetch_layer(): lax.all_gather(second_in, ('fsdp', 'ctx'), axis=0, tiled=True)  258 us
    unnamed x37, waiting for transfers between devices  256 us
    reduce_scatter x1, waiting for transfers between devices, reduce_layer(): lax.psum_scatter(first_in, ('fsdp', 'ctx'), scatter_dimension=0, tiled=True)  134 us
  transfers between devices with their start and end apart: 40, of which 37 were waited for; matrix products, arithmetic and copies ran while one was open for 10% of the time, Pallas kernels for 0%

commit v1 on v0

v1 whole, which is shorter than its diff:
```python
import jax
import jax.numpy as jnp
import numpy as np
from jax import lax
from jax.experimental import pallas as pl
from jax.experimental.pallas import tpu as pltpu
from jax.sharding import Mesh, PartitionSpec as P

F = 16
MAXLEN = 2048

epsilon = 1e-05
quad_scale = 0.7071067811865476
WEIGHT_AXES = ("y", "fsdp", "ctx")
LAYER_AXES = ("fsdp", "ctx")
bf16 = jnp.bfloat16
f32 = jnp.float32


def from_behind(block, axis, distance):
    devices = range(lax.axis_size(axis))
    route = [(i - distance, i) for i in devices if i - distance in devices]
    return lax.ppermute(block, axis, route)


def running_sum(part, direction):
    window = part
    total = jnp.zeros(part.shape, f32)
    step = 1
    while step < lax.axis_size("ctx"):
        arrived = from_behind(window.astype(bf16), "ctx", direction * step).astype(f32)
        total = total + arrived
        window = window + arrived
        step *= 2
    return (total * TIMES[:, None]).astype(bf16)


def sum_everywhere(value):
    for axis in ("core", "y", "fsdp", "ctx"):
        step = 1
        size = lax.axis_size(axis)
        while step < size:
            value = value + lax.ppermute(value, axis, [(i, i ^ step) for i in range(size)])
            step *= 2
    return value


PAIRS = [(a, b) for a in range(F) for b in range(a, F)]
FIRST = np.array([[float(a == i) for a, b in PAIRS] for i in range(F)], np.float32)
SECOND = np.array([[float(b == i) for a, b in PAIRS] for i in range(F)], np.float32)
TIMES = np.array([2.0 if a < b else 1.0 for a, b in PAIRS] + [1.0] * (F + 1), np.float32)


def features(vector):
    quad = jnp.dot(vector, FIRST) * jnp.dot(vector, SECOND) * quad_scale
    return jnp.concatenate([quad, vector, jnp.ones(vector.shape[:-1] + (1,), f32)], axis=-1)


def norm_rows(stream, gain):
    return stream * lax.rsqrt(jnp.mean(stream * stream, axis=-1, keepdims=True) + epsilon) * gain


def slot_index(peer, order_key, per_peer):
    same = peer[:, None] == peer[None, :]
    before = order_key[None, :] < order_key[:, None]
    return peer * per_peer + jnp.sum((same & before).astype(jnp.int32), axis=1)


def regroup(rows, order, position):
    received = lax.all_to_all(
        rows[order], ("ctx", "y", "core"), split_axis=0, concat_axis=0, tiled=True
    )
    return received[position]


def core_swap(value):
    return lax.ppermute(value, "core", [(0, 1), (1, 0)])


def gather_weight(weight):
    whole = lax.all_gather(weight, WEIGHT_AXES, axis=0, tiled=True)
    return whole.reshape(lax.axis_size("y"), -1, weight.shape[1])


def gather_slice(weight):
    return lax.all_gather(weight, LAYER_AXES, axis=0, tiled=True)


def scatter_grad(grad, axes):
    flat = grad.astype(bf16).reshape(-1, grad.shape[-1])
    return lax.psum_scatter(flat, axes, scatter_dimension=0, tiled=True).astype(f32)


def tie(*values):
    return lax.optimization_barrier(values)


def after(value, *others):
    for other in others:
        corner = other.reshape((-1,) + other.shape[-2:])[0, :16, :128]
        first = lax.optimization_barrier(corner)[:1, :1].reshape(())
        value = value + (first * 0).astype(value.dtype)
    return value


def bit_of(axis, step):
    return lax.axis_index(axis) // step % 2


def swap(value, axis, step):
    return lax.ppermute(value, axis, [(i, i ^ step) for i in range(lax.axis_size(axis))])


def pick(value, index, dim):
    return lax.dynamic_index_in_dim(value, index, dim, keepdims=False)


def halve_start(value, axis):
    size = lax.axis_size(axis)
    dims = size.bit_length() - 1
    value = value.reshape((2,) * dims + value.shape[1:])
    bit = bit_of(axis, 1)
    return pick(value, bit, dims - 1), swap(pick(value, 1 - bit, dims - 1), axis, 1)


def halve_rest(kept, arrived, axis):
    size = lax.axis_size(axis) // 2
    value = (kept.astype(f32) + arrived.astype(f32)).astype(bf16)
    dims = size.bit_length() - 1
    return halve(value.reshape((size,) + value.shape[dims:]), axis, 2)


def halve(value, axis, done=1):
    size = lax.axis_size(axis) // done
    dims = size.bit_length() - 1
    value = value.reshape((2,) * dims + value.shape[1:])
    for dim in reversed(range(dims)):
        bit = bit_of(axis, done)
        other = swap(pick(value, 1 - bit, dim), axis, done)
        value = (pick(value, bit, dim).astype(f32) + other.astype(f32)).astype(bf16)
        done *= 2
    return value


def half_columns(rows, bit, fsdp):
    width = rows.shape[1] // fsdp
    if fsdp == 2:
        return lax.dynamic_slice_in_dim(rows, bit * width, width, 1)
    parts = rows.reshape(-1, fsdp // 2, 2, width)
    return pick(parts, bit, 2).reshape(-1, fsdp // 2 * width)


def reduce_start(rows, value):
    fsdp = lax.axis_size("fsdp")
    theirs = slice_grad(half_columns(rows, 1 - bit_of("fsdp", 1), fsdp), value)
    return swap(theirs.astype(bf16), "fsdp", 1)


def reduce_middle(rows, value, arrived):
    fsdp, ctx = (lax.axis_size(axis) for axis in LAYER_AXES)
    k = value.shape[-1]
    mine = slice_grad(half_columns(rows, bit_of("fsdp", 1), fsdp), value)
    total = (mine + arrived.astype(f32)).astype(bf16)
    total = halve(total.reshape(fsdp // 2, ctx, -1, k), "fsdp", 2)
    return halve_start(total, "ctx")


def reduce_grad(rows, value, first):
    fsdp, ctx, y = (lax.axis_size(axis) for axis in ("fsdp", "ctx", "y"))
    k = value.shape[-1]
    d = rows.shape[1] // (fsdp * ctx)
    bit = bit_of(first, 1)
    if first == "y":
        parts = value.reshape(y // 2, 2, -1, k)
        theirs = weight_grad(rows, pick(parts, 1 - bit, 1)).astype(bf16)
        mine = weight_grad(rows, pick(parts, bit, 1))
    else:
        theirs = weight_grad(half_columns(rows, 1 - bit, fsdp), value)
        mine = weight_grad(half_columns(rows, bit, fsdp), value)
        theirs = theirs.astype(bf16)
    total = (mine + swap(theirs, first, 1).astype(f32)).astype(bf16)
    if first == "y":
        total = halve(total.reshape(y // 2, fsdp, ctx, d, k), "y", 2)
        total = halve(total, "fsdp")
    else:
        total = total.reshape(y, fsdp // 2, ctx, d, k).swapaxes(0, 1)
        total = halve(halve(total, "fsdp", 2), "y")
    return halve(total, "ctx").astype(f32)


class Rows:
    def __init__(self, row_count, slot_rows):
        self.count = row_count
        self.own_first = row_count % slot_rows == 0
        self.core = lax.axis_index("core")

    def spread(self, own):
        other = core_swap(own)
        if self.own_first:
            return jnp.concatenate([own, other], axis=0)
        low = jnp.where(self.core == 0, own, other)
        high = jnp.where(self.core == 0, other, own)
        return jnp.concatenate([low, high], axis=0)

    def halves(self, value):
        if self.own_first:
            return value[:, : self.count], value[:, self.count :]
        own = lax.dynamic_slice_in_dim(value, self.core * self.count, self.count, 1)
        other = lax.dynamic_slice_in_dim(value, (1 - self.core) * self.count, self.count, 1)
        return own, other

    def collect(self, value, weight):
        own, other = self.halves(value)
        theirs = jnp.einsum("yrk,ydk->rd", other, weight, preferred_element_type=f32).astype(bf16)
        arrived = core_swap(theirs)
        mine = jnp.einsum("yrk,ydk->rd", own, weight, preferred_element_type=f32)
        return mine + arrived.astype(f32)


def spread_wide(own, *meanwhile):
    value = own[None]
    step = 1
    while step < lax.axis_size("y"):
        arrived, *meanwhile = tie(swap(value, "y", step), *meanwhile)
        value = jnp.concatenate([value, arrived], axis=0)
        step *= 2
    other = core_swap(value)
    value = jnp.concatenate([value, other], axis=0).reshape(-1, own.shape[-1])
    return (value, *meanwhile) if meanwhile else value


def products_wide(value, weight):
    y = lax.axis_size("y")
    blocks = value.reshape(2, y, -1, value.shape[-1])
    count = blocks.shape[2]

    def part(block):
        flat = block.reshape(-1, block.shape[-1])
        return jnp.einsum("rk,dk->rd", flat, weight, preferred_element_type=f32)

    far = part(blocks[:, 1:]).reshape(2, y - 1, count, -1)
    far = far[0] + core_swap(far[1].astype(bf16)).astype(f32)
    extra = 0.0
    step = y // 2
    while step > 1:
        arrived = swap(far[step - 1 :].astype(bf16), "y", step).astype(f32)
        extra = extra + arrived[0]
        far = far[: step - 1] + arrived[1:]
        step //= 2
    near = part(blocks[:, 0]).reshape(2, count, -1)
    return far[0].astype(bf16), near[0] + extra, near[1].astype(bf16)


def collect_wide(value, weight, *meanwhile):
    far, near, neighbour = products_wide(value, weight)
    arrived, near, neighbour, *meanwhile = tie(swap(far, "y", 1), near, neighbour, *meanwhile)
    total = near + core_swap(neighbour).astype(f32) + arrived.astype(f32)
    return (total, *meanwhile) if meanwhile else total


def slice_project(rows, weight):
    return jnp.einsum("rd,dk->rk", rows, weight, preferred_element_type=f32)


def slice_grad(rows, value):
    return jnp.einsum("rd,rk->dk", rows, value, preferred_element_type=f32)


def project(normed, weight):
    return jnp.einsum("rd,ydk->yrk", normed, weight, preferred_element_type=f32)


def weight_grad(rows, value):
    return jnp.einsum("rd,yrk->ydk", rows, value, preferred_element_type=f32)


def split_sequences(value, slot_rows):
    return value.reshape(value.shape[0], -1, slot_rows, value.shape[-1])


def join_sequences(value):
    return value.reshape(value.shape[0], -1, value.shape[-1])


def conv_forward(normed, w_in, kernel, slot_rows):
    z = split_sequences(project(normed, w_in), slot_rows)
    ch = z.shape[-1] // 2
    signal = z[..., :ch].astype(bf16)
    gate = z[..., ch:]
    before = from_behind(signal[:, :, slot_rows - 2 :], "ctx", 1)
    widened = jnp.concatenate([before, signal], axis=2).astype(f32)
    taps = (widened[:, :, 2:], widened[:, :, 1:-1], widened[:, :, :-2])
    k = kernel[:, :, None, None, :]
    mixture = k[0] * taps[0] + k[1] * taps[1] + k[2] * taps[2]
    hidden = join_sequences((mixture * gate).astype(bf16))
    return hidden, (widened.astype(bf16), gate)


def conv_backward(grad_out, w_out, kernel, stored, slot_rows):
    widened, gate = stored
    widened = widened.astype(f32)
    taps = (widened[:, :, 2:], widened[:, :, 1:-1], widened[:, :, :-2])
    k = kernel[:, :, None, None, :]
    mixture = k[0] * taps[0] + k[1] * taps[1] + k[2] * taps[2]
    grad_hidden = split_sequences(project(grad_out, w_out), slot_rows)
    grad_mix = grad_hidden * gate
    grad_gate = grad_hidden * mixture
    after = from_behind(grad_mix[:, :, :2], "ctx", -1)
    wide = jnp.concatenate([grad_mix, after], axis=2)
    grad_signal = k[0] * grad_mix + k[1] * wide[:, :, 1:-1] + k[2] * wide[:, :, 2:]
    grad_kernel = jnp.stack([jnp.sum(grad_mix * tap, axis=(1, 2)) for tap in taps])
    grad_signal = join_sequences(grad_signal.astype(bf16))
    grad_gate = join_sequences(grad_gate.astype(bf16))
    return grad_signal, grad_gate, grad_kernel


def ffn_forward(normed, w_in):
    z = lax.optimization_barrier(slice_project(normed, w_in).astype(bf16))
    f = z.shape[-1] // 2
    hidden = (jax.nn.silu(z[..., :f].astype(f32)) * z[..., f:].astype(f32)).astype(bf16)
    return hidden, z


def swiglu_grad_kernel(grad_ref, weight_ref, z_ref, out_ref):
    f = weight_ref.shape[1]
    grad_hidden = jnp.dot(grad_ref[...], weight_ref[...], preferred_element_type=f32)
    z = z_ref[...].astype(f32)
    gate, up = z[:, :f], z[:, f:]
    s = 1.0 / (1.0 + jnp.exp(-gate))
    out_ref[:, :f] = (grad_hidden * up * (s * (1.0 + gate * (1.0 - s)))).astype(bf16)
    out_ref[:, f:] = (grad_hidden * (gate * s)).astype(bf16)


def ffn_backward(grad_out, w_out, z):
    count, width = grad_out.shape
    f = w_out.shape[1]
    block = 256
    return pl.pallas_call(
        swiglu_grad_kernel,
        grid=(count // block,),
        in_specs=[
            pl.BlockSpec((block, width), lambda i: (i, 0)),
            pl.BlockSpec((width, f), lambda i: (0, 0)),
            pl.BlockSpec((block, 2 * f), lambda i: (i, 0)),
        ],
        out_specs=pl.BlockSpec((block, 2 * f), lambda i: (i, 0)),
        out_shape=jax.ShapeDtypeStruct((count, 2 * f), bf16),
        cost_estimate=pl.CostEstimate(
            flops=2 * count * width * f,
            bytes_accessed=2 * (count * width + width * f + 4 * count * f),
            transcendentals=count * f,
        ),
        compiler_params=pltpu.CompilerParams(vmem_limit_bytes=56 * 2**20),
    )(grad_out, w_out, z)


def pair_grad_kernel(rows_ref, first_ref, grad_ref, second_ref, out_ref):
    split = first_ref.shape[1]
    down = (((0,), (0,)), ((), ()))
    out_ref[:, :split] = lax.dot_general(
        rows_ref[...], first_ref[...], down, preferred_element_type=f32
    ).astype(bf16)
    out_ref[:, split:] = lax.dot_general(
        grad_ref[...], second_ref[...], down, preferred_element_type=f32
    ).astype(bf16)


def pair_grad(rows, first, grad, second):
    count, width = rows.shape
    a, b = first.shape[1], second.shape[1]
    block = 256
    return pl.pallas_call(
        pair_grad_kernel,
        grid=(width // block,),
        in_specs=[
            pl.BlockSpec((count, block), lambda i: (0, i)),
            pl.BlockSpec((count, a), lambda i: (0, 0)),
            pl.BlockSpec((count, block), lambda i: (0, i)),
            pl.BlockSpec((count, b), lambda i: (0, 0)),
        ],
        out_specs=pl.BlockSpec((block, a + b), lambda i: (i, 0)),
        out_shape=jax.ShapeDtypeStruct((width, a + b), bf16),
        cost_estimate=pl.CostEstimate(
            flops=2 * count * width * (a + b),
            bytes_accessed=2 * (2 * count * width + (count + width) * (a + b)),
            transcendentals=0,
        ),
        compiler_params=pltpu.CompilerParams(vmem_limit_bytes=56 * 2**20),
    )(rows, first, grad, second)


def causal_mask(slot_rows):
    return jnp.arange(slot_rows)[:, None] >= jnp.arange(slot_rows)[None, :]


def to_heads(z, heads):
    y, s, l, width = z.shape
    return z.reshape(y, s, l, heads, width // heads).transpose(0, 1, 3, 2, 4)


def from_heads(value):
    y, s, h, l, e = value.shape
    return value.transpose(0, 1, 3, 2, 4).reshape(y, s * l, h * e)


def attn_forward(normed, w_in, heads, slot_rows):
    z = split_sequences(project(normed, w_in), slot_rows)
    queries = to_heads((0.5 * z[..., : heads * F]).astype(bf16), heads)
    keys = to_heads((0.5 * z[..., heads * F : 2 * heads * F]).astype(bf16), heads)
    values = to_heads(z[..., 2 * heads * F :].astype(bf16), heads)
    extended = jnp.concatenate([values, jnp.ones(values.shape[:-1] + (1,), bf16)], axis=-1)
    k_feat = features(keys.astype(f32)).astype(bf16)
    states = jnp.einsum("...qe,...qv->...ev", k_feat, extended, preferred_element_type=f32)
    earlier = running_sum(states, 1)
    scores = jnp.einsum("...pf,...qf->...pq", queries, keys, preferred_element_type=f32)
    weight = jnp.where(
        causal_mask(slot_rows), 1.0 + scores + 0.5 * scores * scores, 0.0
    ).astype(bf16)
    q_feat = features(queries.astype(f32)).astype(bf16)
    totals = jnp.einsum(
        "...pq,...qv->...pv", weight, extended, preferred_element_type=f32
    ) + jnp.einsum("...pe,...ev->...pv", q_feat, earlier, preferred_element_type=f32)
    out = from_heads((totals[..., :-1] / totals[..., -1:]).astype(bf16))
    return out, (queries, keys, extended, earlier, totals)


def attn_backward(grad_out, w_out, stored, heads, slot_rows):
    (queries, keys, extended, earlier, totals), grad_out = lax.optimization_barrier(
        (stored, grad_out)
    )
    q_feat = features(queries.astype(f32)).astype(bf16)
    k_feat = features(keys.astype(f32)).astype(bf16)
    grad_heads = to_heads(split_sequences(project(grad_out, w_out), slot_rows), heads)
    denominator = totals[..., -1:]
    grad_num = grad_heads / denominator
    grad_den = -jnp.sum(grad_heads * totals[..., :-1], axis=-1, keepdims=True) / (
        denominator * denominator
    )
    grad_total = jnp.concatenate([grad_num, grad_den], axis=-1).astype(bf16)
    grad_prior = jnp.einsum("...pe,...pv->...ev", q_feat, grad_total, preferred_element_type=f32)
    grad_state = running_sum(grad_prior, -1)
    scores = jnp.einsum("...pf,...qf->...pq", queries, keys, preferred_element_type=f32)
    mask = causal_mask(slot_rows)
    weight = jnp.where(mask, 1.0 + scores + 0.5 * scores * scores, 0.0).astype(bf16)
    grad_weight = jnp.einsum("...pv,...qv->...pq", grad_total, extended, preferred_element_type=f32)
    grad_qf = jnp.einsum("...pv,...ev->...pe", grad_total, earlier, preferred_element_type=f32)
    grad_score = jnp.where(mask, grad_weight * (1.0 + scores), 0.0).astype(bf16)
    grad_ext = jnp.einsum(
        "...pq,...pv->...qv", weight, grad_total, preferred_element_type=f32
    ) + jnp.einsum("...qe,...ev->...qv", k_feat, grad_state, preferred_element_type=f32)
    grad_kf = jnp.einsum("...qv,...ev->...qe", extended, grad_state, preferred_element_type=f32)
    unused, pull_query = jax.vjp(features, queries.astype(f32))
    unused, pull_key = jax.vjp(features, keys.astype(f32))
    grad_query = (
        jnp.einsum("...pq,...qf->...pf", grad_score, keys, preferred_element_type=f32)
        + pull_query(grad_qf)[0]
    )
    grad_key = (
        jnp.einsum("...pq,...pf->...qf", grad_score, queries, preferred_element_type=f32)
        + pull_key(grad_kf)[0]
    )
    grad_z = jnp.concatenate(
        [
            from_heads((0.5 * grad_query).astype(bf16)),
            from_heads((0.5 * grad_key).astype(bf16)),
            from_heads(grad_ext[..., :-1].astype(bf16)),
        ],
        axis=-1,
    )
    return grad_z


def norm_back(stream, grad_normed, gain):
    unused, pull = jax.vjp(norm_rows, stream, gain)
    return pull(grad_normed)


def heads_apart(weight):
    d = weight.shape[0]
    return jnp.concatenate(
        [
            weight[..., :F].reshape(d, -1),
            weight[..., F : 2 * F].reshape(d, -1),
            weight[..., 2 * F :].reshape(d, -1),
        ],
        axis=1,
    )


def heads_together(weight, heads):
    d = weight.shape[0]
    q = weight[:, : heads * F].reshape(d, heads, F)
    k = weight[:, heads * F : 2 * heads * F].reshape(d, heads, F)
    v = weight[:, 2 * heads * F :].reshape(d, heads, -1)
    return jnp.concatenate([q, k, v], axis=-1)


def shards(
    hidden_in,
    cotangent,
    lengths,
    to_model,
    to_loader,
    conv_in,
    conv_kernel,
    conv_out,
    ffn_one_in,
    ffn_one_out,
    attn_in,
    attn_out,
    ffn_two_in,
    ffn_two_out,
    gains,
):
    y_size = lax.axis_size("y")
    ctx_size = lax.axis_size("ctx")
    tp_size = 2 * y_size
    group_size = ctx_size * tp_size
    row_count = hidden_in.shape[0]
    per_peer = row_count // group_size
    slot_rows = MAXLEN // ctx_size
    block_rows = row_count * tp_size
    core = lax.axis_index("core")
    tp_rank = lax.axis_index("y") * 2 + core
    heads = attn_in.shape[1]
    rows = Rows(row_count, slot_rows)

    d = conv_in.shape[0]
    conv_width = conv_in.shape[1] * conv_in.shape[2]
    attn_width = heads * attn_in.shape[2]
    attn_start = -(-attn_width // 128) * 128
    c_w = gather_weight(jnp.concatenate([conv_in.reshape(d, -1), conv_out.T], axis=1))
    pad = jnp.zeros((d, attn_start - attn_width), bf16)
    a_w = jnp.concatenate([heads_apart(attn_in), pad, attn_out.T], axis=1)
    ffn_width = ffn_one_in.shape[1] * ffn_one_in.shape[2]
    f1_w = jnp.concatenate([ffn_one_in.reshape(d, -1), ffn_one_out.T], axis=1)
    f2_w = jnp.concatenate([ffn_two_in.reshape(d, -1), ffn_two_out.T], axis=1)

    counter = jnp.arange(row_count, dtype=jnp.int32)
    send_slot = slot_index(to_loader // row_count % group_size, counter, per_peer)
    recv_slot = slot_index(to_model // row_count % group_size, to_model % row_count, per_peer)
    send_order = jnp.argsort(send_slot)
    stream_zero = regroup(hidden_in, send_order, recv_slot)
    f1_w = gather_slice(after(f1_w, c_w, stream_zero))
    a_w = gather_weight(after(a_w, f1_w))
    f2_w = gather_slice(after(f2_w, a_w))
    cotangent = after(cotangent, stream_zero)
    w_c_in, w_c_out = c_w[..., :conv_width], c_w[..., conv_width:]
    w_a_in, w_a_out = a_w[..., :attn_width], a_w[..., attn_start:]
    w_f1_in, w_f1_out = f1_w[:, :ffn_width], f1_w[:, ffn_width:]
    w_f2_in, w_f2_out = f2_w[:, :ffn_width], f2_w[:, ffn_width:]
    cotan_rows = regroup(cotangent, send_order, recv_slot)
    stream_zero = stream_zero.astype(f32)
    seq_lengths = lax.dynamic_index_in_dim(lengths, lax.axis_index("fsdp"), 0, keepdims=False)
    position = lax.axis_index("ctx") * slot_rows + jnp.arange(slot_rows, dtype=jnp.int32)
    valid_block = (position[None, :] < seq_lengths[:, None]).astype(f32).reshape(block_rows)
    valid_rows = lax.dynamic_slice_in_dim(valid_block, tp_rank * row_count, row_count)[:, None]
    channels = conv_in.shape[2]
    kernel = lax.dynamic_index_in_dim(
        conv_kernel.reshape(3, y_size, 2, channels), core, 2, keepdims=False
    )

    def normed_of(stream, index, spread=rows.spread):
        return spread(norm_rows(stream, gains[index]).astype(bf16))

    def grad_rows(carry, spread=rows.spread, *meanwhile):
        return spread((valid_rows * carry).astype(bf16), *meanwhile)

    normed_zero = normed_of(stream_zero, 0)
    hid_zero, stored_zero = conv_forward(normed_zero, w_c_in, kernel, slot_rows)
    stream_one = stream_zero + valid_rows * rows.collect(hid_zero, w_c_out)
    normed_one = normed_of(stream_one, 1, spread_wide)
    upstream = cotan_rows.astype(f32)
    normed_one, grad_out = tie(normed_one, grad_rows(upstream, spread_wide))
    hid_one, z_one = ffn_forward(normed_one, w_f1_in)
    stream_two = stream_one + valid_rows * collect_wide(hid_one, w_f1_out)
    normed_two = normed_of(stream_two, 2)
    hid_two, stored_two = attn_forward(normed_two, w_a_in, heads, slot_rows)
    stream_three = stream_two + valid_rows * rows.collect(hid_two, w_a_out)
    normed_three = normed_of(stream_three, 3, spread_wide)
    hid_three, z_three = ffn_forward(normed_three, w_f2_in)

    grad_z = ffn_backward(grad_out, w_f2_out, z_three)
    g_f2 = pair_grad(normed_three, grad_z, grad_out, hid_three)
    terms, g_f2 = collect_wide(grad_z, w_f2_in, g_f2)
    step, gain_three = norm_back(stream_three, terms, gains[3])
    upstream = upstream + step
    grad_out = grad_rows(upstream)
    grad_z = attn_backward(grad_out, w_a_out, stored_two, heads, slot_rows)
    g_f2 = scatter_grad(g_f2, LAYER_AXES)
    g_f2_in, g_f2_out = g_f2[:, :ffn_width], g_f2[:, ffn_width:]
    g_a_out = reduce_grad(grad_out, hid_two, "fsdp")
    g_a_in = reduce_grad(normed_two, grad_z, "y")
    step, gain_two = norm_back(stream_two, rows.collect(grad_z, w_a_in), gains[2])
    upstream = upstream + step
    upstream, hid_three = tie(upstream, hid_three)
    last_terms = products_wide(hid_three, w_f2_out)
    grad_out, *last_terms = grad_rows(upstream, spread_wide, *last_terms)
    out_arrived = reduce_start(grad_out, hid_one)
    grad_z = ffn_backward(grad_out, w_f1_out, z_one)
    in_arrived = reduce_start(normed_one, grad_z)
    step, gain_one = norm_back(stream_one, collect_wide(grad_z, w_f1_in), gains[1])
    upstream = upstream + step
    own_rows = (valid_rows * upstream).astype(bf16)
    own_rows, out_arrived, *last_terms = tie(own_rows, out_arrived, *last_terms)
    last_arrived = swap(last_terms[0], "y", 1)
    stream_four = last_terms[1] + core_swap(last_terms[2]).astype(f32) + last_arrived.astype(f32)
    stream_four = stream_three + valid_rows * stream_four
    hidden_out = regroup(stream_four.astype(bf16), jnp.argsort(recv_slot), send_slot)
    out_parts = reduce_middle(grad_out, hid_one, out_arrived)
    grad_out = rows.spread(own_rows)
    g_c_out = reduce_grad(grad_out, hid_zero, "fsdp")
    grad_signal, grad_gate, grad_kernel = conv_backward(
        grad_out, w_c_out, kernel, stored_zero, slot_rows
    )
    g_c_gate = reduce_grad(normed_zero, grad_gate, "y")
    grad_signal, in_arrived, g_a_in, g_a_out, *out_parts = tie(
        grad_signal, in_arrived, g_a_in, g_a_out, *out_parts
    )
    g_f1_out = halve_rest(*out_parts, "ctx").astype(f32)
    g_f1_in = halve_rest(*reduce_middle(normed_one, grad_z, in_arrived), "ctx").astype(f32)
    g_c_signal = reduce_grad(normed_zero, grad_signal, "fsdp")
    grad_z = jnp.concatenate([grad_signal, grad_gate], axis=-1)
    step, gain_zero = norm_back(stream_zero, rows.collect(grad_z, w_c_in), gains[0])
    upstream = upstream + step
    grad_in = regroup(upstream.astype(bf16), jnp.argsort(recv_slot), send_slot)

    kernel_full = jnp.where(
        (jnp.arange(2) == core)[None, None, :, None], grad_kernel[:, :, None, :], 0.0
    ).reshape(conv_kernel.shape)
    gain_stack = jnp.stack([gain_zero, gain_one, gain_two, gain_three])
    summed = sum_everywhere(jnp.concatenate([gain_stack, kernel_full], axis=0))
    return (
        hidden_out,
        grad_in,
        jnp.stack([g_c_signal, g_c_gate], axis=1),
        summed[4:],
        g_c_out.T,
        g_f1_in.reshape(ffn_one_in.shape),
        g_f1_out.T,
        heads_together(g_a_in, heads),
        g_a_out.T,
        g_f2_in.reshape(ffn_two_in.shape),
        g_f2_out.T,
        summed[:4],
    )


def solution(mesh):
    fsdp, ctx, tp = mesh.devices.shape
    fine = Mesh(mesh.devices.reshape(fsdp, ctx, tp // 2, 2), ("fsdp", "ctx", "y", "core"))
    everything = ("fsdp", "ctx", "y", "core")
    layer = ("fsdp", "ctx")
    tensor = ("y", "core")
    ins = (
        P(everything, None),
        P(everything, None),
        P(),
        P(everything),
        P(everything),
        P(layer, None, tensor),
        P(),
        P(tensor, layer),
        P(layer, None, tensor),
        P(tensor, layer),
        P(layer, tensor, None),
        P(tensor, layer),
        P(layer, None, tensor),
        P(tensor, layer),
        P(),
    )
    outs = (
        P(everything, None),
        P(everything, None),
        P(layer, None, tensor),
        P(),
        P(tensor, layer),
        P(layer, None, tensor),
        P(tensor, layer),
        P(layer, tensor, None),
        P(tensor, layer),
        P(layer, None, tensor),
        P(tensor, layer),
        P(),
    )
    return jax.shard_map(shards, mesh=fine, in_specs=ins, out_specs=outs, check_vma=False)
```

time: 4140 us -> 1890 us (0.46)
  waiting for transfers between devices: 3260 us -> 864 us
  local copies, waits for them, and re-layouts: 159 us -> 267 us
  Pallas kernels: 0 us -> 75.8 us
  matrix products: 459 us -> 387 us
  starting transfers between devices: 51.9 us -> 99.4 us
  blocking collectives: 44.2 us -> 0 us
    reduce_scatter x13 -> x1, waiting for transfers between devices: 1700 us -> 0.01 us  [scatter_grad(): lax.psum_scatter(flat, axes, scatter_dimension=0, tiled=True).astype(f32)]
    all_gather x18 -> x4, waiting for transfers between devices: 1160 us -> 216 us  [the longest x2 163 us: gather_weight(): whole = lax.all_gather(weight, WEIGHT_AXES, axis=0, tiled=True)]
    ppermute x0 -> x59, waiting for transfers between devices: none -> 446 us  [the longest x34 410 us: swap(): lax.ppermute(value, axis, [(i, i ^ step) for i in range(lax.axis_size(axi...]
    unnamed x37 -> x5, waiting for transfers between devices: 256 us -> 0.08 us
    ppermute x2 -> x6, waiting for transfers between devices: 1.82 us -> 145 us  [from_behind(): return lax.ppermute(block, axis, route)]
    all_to_all x4, waiting for transfers between devices: 147 us -> 57.2 us  [regroup(): lax.all_to_all(rows[order], ('ctx', 'y', 'core'), split_axis=0, concat_ax...]
    pallas_call x0 -> x3, Pallas kernels: none -> 75.8 us  [the longest x2 38.4 us: ffn_backward(): pl.pallas_call(swiglu_grad_kernel, grid=(count // block,), in_specs=[pl.B...]
    ppermute x0 -> x59, starting transfers between devices: none -> 60.9 us  [the longest x34 53.3 us: swap(): lax.ppermute(value, axis, [(i, i ^ step) for i in range(lax.axis_size(axi...]
  transfers between devices with their start and end apart: 40 -> 74, of which waited for: 37 -> 38; matrix products, arithmetic and copies ran while one was open for 10% -> 33% of each run, Pallas kernels for 0% -> 3%
where the time goes in v1:
time: 1890 us; the launch traced here: 1870 us
  waiting for transfers between devices  864 us (46%)
  matrix products  387 us (20%)
  local copies, waits for them, and re-layouts  267 us (14%)
  other arithmetic  162 us (9%)
  starting transfers between devices  99.4 us (5%)
  Pallas kernels  75.8 us (4%)
  between operations  19.2 us (1%)
    ppermute x34, waiting for transfers between devices, swap(): lax.ppermute(value, axis, [(i, i ^ step) for i in range(lax.axis_size(axi...  410 us
    all_gather x2, waiting for transfers between devices, gather_weight(): whole = lax.all_gather(weight, WEIGHT_AXES, axis=0, tiled=True)  163 us
    ppermute x6, waiting for transfers between devices, from_behind(): return lax.ppermute(block, axis, route)  145 us
    dot_general x8, matrix products, part(): return jnp.einsum('rk,dk->rd', flat, weight, preferred_element_type=f32)  90.3 us
    all_to_all x4, waiting for transfers between devices, regroup(): lax.all_to_all(rows[order], ('ctx', 'y', 'core'), split_axis=0, concat_ax...  57.2 us
    all_gather x2, waiting for transfers between devices, gather_slice(): return lax.all_gather(weight, LAYER_AXES, axis=0, tiled=True)  53.4 us
    ppermute x34, starting transfers between devices, swap(): lax.ppermute(value, axis, [(i, i ^ step) for i in range(lax.axis_size(axi...  53.3 us
    dot_general x10, matrix products, weight_grad(): return jnp.einsum('rd,yrk->ydk', rows, value, preferred_element_type=f32)  50.8 us
  transfers between devices with their start and end apart: 74, of which 38 were waited for; matrix products, arithmetic and copies ran while one was open for 33% of the time, Pallas kernels for 3%

profile of v1, /device:TPU:0, one launch (start us, length us, event | category | flops | bytes accessed | tf_op | source)
XLA Modules:
  0.0 1873.7 jit_solution(16790869224659253580)
XLA Ops:
  30.3 57.2 %all-to-all-done = bf16[16,32,1792]{2,1,0:T(8,128)(2,1)S(1)} async-done(((bf16[16,32,1792]{2,1,0:T(8,128)(2,1)}), bf16[16,32,1792]{2,1,0:T(8,128)(2,1)S(1)}, u32[]{:S(2)}, u32[]{:S(2)}) %all-to-all-start) | async-done | bytes 1835040 | tf_op jit(solution)/shard_map/all_to_all | solution.py:70
  92.6 79.6 %all-gather.5.cloned.1.call-done = bf16[3584,1344]{1,0:T(8,128)(2,1)} async-done(((bf16[224,1344]{1,0:T(8,128)(2,1)}), bf16[3584,1344]{1,0:T(8,128)(2,1)}) %all-gather.5.cloned.1.call-update) | async-done | bytes 9633808 | tf_op jit(solution)/shard_map/all_gather | solution.py:81
  215.7 32.6 %collective-permute-done.1 = bf16[2,2,2,448]{3,2,1,0:T(2,128)(2,1)S(1)} collective-permute-done((bf16[2,2,2,448]{3,2,1,0:T(2,128)(2,1)S(1)}, bf16[2,2,2,448]{3,2,1,0:T(2,128)(2,1)S(1)}, u32[]{:S(2)}, u32[]{:S(2)}) %collective-permute-start.1) | collective-permute-done | bytes 7200 | tf_op jit(solution)/shard_map/ppermute | solution.py:23
  275.1 33.3 %collective-permute-done.5 = bf16[1,512,1792]{2,1,0:T(8,128)(2,1)S(1)} collective-permute-done((bf16[1,512,1792]{2,1,0:T(8,128)(2,1)S(1)}, bf16[1,512,1792]{2,1,0:T(8,128)(2,1)S(1)}, u32[]{:S(2)}, u32[]{:S(2)}) %collective-permute-start.5) | collective-permute-done | bytes 1835040 | tf_op jit(solution)/shard_map/ppermute | solution.py:111
  311.4 36.2 %collective-permute-done.3 = bf16[1,512,1792]{2,1,0:T(8,128)(2,1)S(1)} collective-permute-done((bf16[1,512,1792]{2,1,0:T(8,128)(2,1)S(1)}, bf16[1,512,1792]{2,1,0:T(8,128)(2,1)S(1)}, u32[]{:S(2)}, u32[]{:S(2)}) %collective-permute-start.3) | collective-permute-done | bytes 1835040 | tf_op jit(solution)/shard_map/ppermute | solution.py:111
  351.4 46.9 %all-gather.7.cloned.1.call-done = bf16[1792,3648]{1,0:T(8,128)(2,1)} async-done(((bf16[224,3648]{1,0:T(8,128)(2,1)}), bf16[1792,3648]{1,0:T(8,128)(2,1)}) %all-gather.7.cloned.1.call-update) | async-done | bytes 13074448 | tf_op jit(solution)/shard_map/all_gather | solution.py:86
  411.3 23.3 %convolution_convert_fusion.1.z_ref = bf16[2048,2432]{1,0:T(8,128)(2,1)S(1)} fusion(bf16[2048,1792]{1,0:T(8,128)(2,1)S(1)} %bitcast.530, bf16[1792,3648]{1,0:T(8,128)(2,1)} %all-gather.7.cloned.1.call-done), kind=kOutput, calls=%fused_computation.22 | convolution fusion | flops 17855938560 | bytes 26017792 | tf_op jit(solution)/shard_map/rd,dk->rk/dot_general | solution.py:262
  458.3 83.0 %all-gather.9.cloned.1.call-done = bf16[3584,1088]{1,0:T(8,128)(2,1)} async-done(((bf16[224,1088]{1,0:T(8,128)(2,1)}), bf16[3584,1088]{1,0:T(8,128)(2,1)}) %all-gather.9.cloned.1.call-update) | async-done | bytes 7798800 | tf_op jit(solution)/shard_map/all_gather | solution.py:81
  593.6 26.8 %collective-permute-done.11 = bf16[2,2,4,153,113]{4,2,3,1,0:T(4,128)(2,1)S(1)} collective-permute-done((bf16[2,2,4,153,113]{4,2,3,1,0:T(4,128)(2,1)S(1)}, bf16[2,2,4,153,113]{4,2,3,1,0:T(4,128)(2,1)S(1)}, u32[]{:S(2)}, u32[]{:S(2)}) %collective-permute-start.11) | collective-permute-done | bytes 553280 | tf_op jit(solution)/shard_map/ppermute | solution.py:23
  628.2 25.3 %collective-permute-done.12 = bf16[2,2,4,153,113]{4,2,3,1,0:T(4,128)(2,1)S(1)} collective-permute-done((bf16[2,2,4,153,113]{4,2,3,1,0:T(4,128)(2,1)S(1)}, bf16[2,2,4,153,113]{4,2,3,1,0:T(4,128)(2,1)S(1)}, u32[]{:S(2)}, u32[]{:S(2)}) %collective-permute-start.12) | collective-permute-done | bytes 553280 | tf_op jit(solution)/shard_map/ppermute | solution.py:23
  689.8 40.6 %collective-permute-done.14 = bf16[1,512,1792]{2,1,0:T(8,128)(2,1)S(1)} collective-permute-done((bf16[1,512,1792]{2,1,0:T(8,128)(2,1)S(1)}, bf16[1,512,1792]{2,1,0:T(8,128)(2,1)S(1)}, u32[]{:S(2)}, u32[]{:S(2)}) %collective-permute-start.14) | collective-permute-done | bytes 1835040 | tf_op jit(solution)/shard_map/ppermute | solution.py:111
  747.2 25.3 %convolution_convert_fusion.z_ref = bf16[2048,2432]{1,0:T(8,128)(2,1)} fusion(bf16[2048,1792]{1,0:T(8,128)(2,1)} %bitcast.542, bf16[1792,3648]{1,0:T(8,128)(2,1)} %all-gather.11.cloned.1.call-done), kind=kOutput, calls=%fused_computation.21 | convolution fusion | flops 17855938560 | bytes 26017792 | tf_op jit(solution)/shard_map/rd,dk->rk/dot_general | solution.py:262
  777.3 19.2 %shard_map.274.first_ref = bf16[2048,2432]{1,0:T(8,128)(2,1)} custom-call(bf16[2048,1792]{1,0:T(8,128)(2,1)} %bitcast.535, bf16[1792,1216]{1,0:T(8,128)(2,1)} %slice.443.weight_ref, bf16[2048,2432]{1,0:T(8,128)(2,1)} %convolution_convert_fusion.z_ref), custom_call_target="tpu_custom_call" | custom-call | flops 8925478912 | bytes 31621120 | tf_op jit(solution)/shard_map/pallas_call | solution.py:338
  852.0 37.4 %shard_map.275 = bf16[1792,3648]{1,0:T(8,128)(2,1)} custom-call(bf16[2048,1792]{1,0:T(8,128)(2,1)} %bitcast.543, bf16[2048,2432]{1,0:T(8,128)(2,1)} %shard_map.274.first_ref, bf16[2048,1792]{1,0:T(8,128)(2,1)} %bitcast.536, bf16[2048,1216]{1,0:T(8,128)(2,1)} %fusion.14.second_ref), custom_call_target="tpu_custom_call" | custom-call | flops 26776436736 | bytes 42696704 | tf_op jit(solution)/shard_map/pallas_call | solution.py:372
  1001.9 43.8 %collective-permute-done.21 = bf16[2,2,4,153,113]{4,2,3,1,0:T(4,128)(2,1)S(1)} collective-permute-done((bf16[2,2,4,153,113]{4,2,3,1,0:T(4,128)(2,1)S(1)}, bf16[2,2,4,153,113]{4,2,3,1,0:T(4,128)(2,1)S(1)}, u32[]{:S(2)}, u32[]{:S(2)}) %collective-permute-start.21) | collective-permute-done | bytes 553280 | tf_op jit(solution)/shard_map/ppermute | solution.py:23
  1112.0 24.0 %collective-permute-done.23 = bf16[1,512,1792]{2,1,0:T(8,128)(2,1)S(1)} collective-permute-done((bf16[1,512,1792]{2,1,0:T(8,128)(2,1)S(1)}, bf16[1,512,1792]{2,1,0:T(8,128)(2,1)S(1)}, u32[]{:S(2)}, u32[]{:S(2)}) %collective-permute-start.23) | collective-permute-done | bytes 1835040 | tf_op jit(solution)/shard_map/ppermute | solution.py:111
  1169.3 42.6 %collective-permute-done.40 = bf16[4,224,448]{2,1,0:T(8,128)(2,1)} collective-permute-done((bf16[4,224,448]{2,1,0:T(8,128)(2,1)}, bf16[4,224,448]{2,1,0:T(8,128)(2,1)}, u32[]{:S(2)}, u32[]{:S(2)}) %collective-permute-start.40) | collective-permute-done | bytes 802848 | tf_op jit(solution)/shard_map/ppermute | solution.py:111
  1232.5 19.2 %shard_map.276 = bf16[2048,2432]{1,0:T(8,128)(2,1)} custom-call(bf16[2048,1792]{1,0:T(8,128)(2,1)} %bitcast.537, bf16[1792,1216]{1,0:T(8,128)(2,1)} %slice.424.weight_ref, bf16[2048,2432]{1,0:T(8,128)(2,1)} %copy-done.36), custom_call_target="tpu_custom_call" | custom-call | flops 8925478912 | bytes 31621120 | tf_op jit(solution)/shard_map/pallas_call | solution.py:338
  1387.3 47.7 %collective-permute-done.29 = bf16[896,1216]{0,1:T(8,128)(2,1)} collective-permute-done((bf16[896,1216]{0,1:T(8,128)(2,1)}, bf16[896,1216]{0,1:T(8,128)(2,1)}, u32[]{:S(2)}, u32[]{:S(2)}) %collective-permute-start.29) | collective-permute-done | bytes 2179104 | tf_op jit(solution)/shard_map/ppermute | solution.py:111
  1457.5 20.2 %collective-permute-done.31 = bf16[512,1792]{1,0:T(8,128)(2,1)} collective-permute-done((bf16[512,1792]{1,0:T(8,128)(2,1)}, bf16[512,1792]{1,0:T(8,128)(2,1)}, u32[]{:S(2)}, u32[]{:S(2)}) %collective-permute-start.31) | collective-permute-done | bytes 1835040 | tf_op jit(solution)/shard_map/ppermute | solution.py:111
  1539.8 29.2 %collective-permute-done.34 = bf16[896,2432]{1,0:T(8,128)(2,1)} collective-permute-done((bf16[896,2432]{1,0:T(8,128)(2,1)}, bf16[896,2432]{1,0:T(8,128)(2,1)}, u32[]{:S(2)}, u32[]{:S(2)}) %collective-permute-start.34) | collective-permute-done | bytes 4358176 | tf_op jit(solution)/shard_map/ppermute | solution.py:111
  1734.7 20.9 %collective-permute-done.60 = bf16[2,224,448]{2,1,0:T(8,128)(2,1)} collective-permute-done((bf16[2,224,448]{2,1,0:T(8,128)(2,1)S(1)}, bf16[2,224,448]{2,1,0:T(8,128)(2,1)}, u32[]{:S(2)}, u32[]{:S(2)}) %collective-permute-start.60) | collective-permute-done | bytes 401440 | tf_op jit(solution)/shard_map/ppermute | solution.py:111
  1760.2 34.8 %collective-permute-done.51 = bf16[2,224,448]{2,1,0:T(8,128)(2,1)S(1)} collective-permute-done((bf16[2,224,448]{2,1,0:T(8,128)(2,1)S(1)}, bf16[2,224,448]{2,1,0:T(8,128)(2,1)S(1)}, u32[]{:S(2)}, u32[]{:S(2)}) %collective-permute-start.51) | collective-permute-done | bytes 401440 | tf_op jit(solution)/shard_map/ppermute | solution.py:111
  1808.9 20.1 %collective-permute-done.61 = bf16[224,448]{1,0:T(8,128)(2,1)S(1)} collective-permute-done((bf16[224,448]{1,0:T(8,128)(2,1)S(1)}, bf16[224,448]{1,0:T(8,128)(2,1)S(1)}, u32[]{:S(2)}, u32[]{:S(2)}) %collective-permute-start.61) | collective-permute-done | bytes 200736 | tf_op jit(solution)/shard_map/ppermute | solution.py:111
  (777 shorter events, 985.2 us)
Async XLA Ops:
  7.2 165.0 %all-gather.5.cloned.1.call-start = ((), (), s32[]{:S(2)}) async-start(), calls=%async_computation.5 | async-start | bytes 10723328 | tf_op jit(solution)/shard_map/all_gather | solution.py:81
  28.3 369.9 %all-gather.7.cloned.1.call-start = ((), (), s32[]{:S(2)}) async-start(), calls=%async_computation.6 | async-start | bytes 14966784 | tf_op jit(solution)/shard_map/all_gather | solution.py:86
  184.0 74.6 %all-to-all-start.1 = ((bf16[16,32,1792]{2,1,0:T(8,128)(2,1)}), bf16[16,32,1792]{2,1,0:T(8,128)(2,1)S(1)}, u32[]{:S(2)}, u32[]{:S(2)}) async-start(bf16[16,32,1792]{2,1,0:T(8,128)(2,1)} %bitcast.528), calls=%async_computation.1 | async-start | bytes 3670016 | tf_op jit(solution)/shard_map/all_to_all | solution.py:70
  187.9 353.4 %all-gather.9.cloned.1.call-start = ((), (), s32[]{:S(2)}) async-start(), calls=%async_computation.7 | async-start | bytes 8773632 | tf_op jit(solution)/shard_map/all_gather | solution.py:81
  274.5 73.2 %collective-permute-start.3 = (bf16[1,512,1792]{2,1,0:T(8,128)(2,1)S(1)}, bf16[1,512,1792]{2,1,0:T(8,128)(2,1)S(1)}, u32[]{:S(2)}, u32[]{:S(2)}) collective-permute-start(bf16[1,512,1792]{2,1,0:T(8,128)(2,1)S(1)} %fusion.172), channel_id=1, source_target_pairs={{0,2},{2,0},{1,3},{3,1},{4,6},{6,4},{5,7},{7,5},{8,10},{10,8},{9,1... | collective-permute-start | bytes 5505032 | tf_op jit(solution)/shard_map/ppermute | solution.py:111
  310.8 90.7 %collective-permute-start.6 = (bf16[2,512,1792]{2,1,0:T(8,128)(2,1)}, bf16[2,512,1792]{2,1,0:T(8,128)(2,1)}, u32[]{:S(2)}, u32[]{:S(2)}) collective-permute-start(bf16[2,512,1792]{2,1,0:T(8,128)(2,1)} %pad_maximum_fusion.8), channel_id=1, source_target_pairs={{0,1},{1,0},{2,3},{3,2},{4,5},{5,4},{6,7},{7,6},{8,9},{9,8},{10,11... | collective-permute-start | bytes 11010056 | tf_op jit(solution)/shard_map/ppermute | solution.py:77
  401.0 346.2 %all-gather.11.cloned.1.call-start = ((), (), s32[]{:S(2)}) async-start(), calls=%async_computation.8 | async-start | bytes 14966784 | tf_op jit(solution)/shard_map/all_gather | solution.py:86
  456.1 97.3 %collective-permute-start.8 = (bf16[512,1792]{1,0:T(8,128)(2,1)}, bf16[512,1792]{1,0:T(8,128)(2,1)}, u32[]{:S(2)}, u32[]{:S(2)}) collective-permute-start(bf16[512,1792]{1,0:T(8,128)(2,1)} %fusion.177), channel_id=1, source_target_pairs={{0,2},{2,0},{1,3},{3,1},{4,6},{6,4},{5,7},{7,5},{8,10},{10,8},{9,1... | collective-permute-start | bytes 5505032 | tf_op jit(solution)/shard_map/ppermute | solution.py:111
  544.6 1313.7 %reduce-scatter.2.cloned.1.call-start = ((), (), s32[]{:S(2)}) async-start(), calls=%async_computation.9 | async-start | bytes 14966784 | tf_op jit(solution)/shard_map/reduce_scatter | solution.py:91
  1138.6 87.8 %collective-permute-start.25 = (bf16[2,512,1792]{2,1,0:T(8,128)(2,1)}, bf16[2,512,1792]{2,1,0:T(8,128)(2,1)}, u32[]{:S(2)}, u32[]{:S(2)}) collective-permute-start(bf16[2,512,1792]{2,1,0:T(8,128)(2,1)} %pad_maximum_fusion.11), channel_id=1, source_target_pairs={{0,1},{1,0},{2,3},{3,2},{4,5},{5,4},{6,7},{7,6},{8,9},{9,8},{10,11... | collective-permute-start | bytes 11010056 | tf_op jit(solution)/shard_map/ppermute | solution.py:77
  1144.6 69.2 %collective-permute-start.35 = (bf16[1,1792,576]{1,2,0:T(8,128)(2,1)}, bf16[1,1792,576]{1,2,0:T(8,128)(2,1)}, u32[]{:S(2)}, u32[]{:S(2)}) collective-permute-start(bf16[1,1792,576]{1,2,0:T(8,128)(2,1)} %fusion.120), channel_id=1, source_target_pairs={{0,2},{2,0},{1,3},{3,1},{4,6},{6,4},{5,7},{7,5},{8,10},{10,8},{9,1... | collective-permute-start | bytes 6193160 | tf_op jit(solution)/shard_map/ppermute | solution.py:111
  1356.5 78.5 %collective-permute-start.29 = (bf16[896,1216]{0,1:T(8,128)(2,1)}, bf16[896,1216]{0,1:T(8,128)(2,1)}, u32[]{:S(2)}, u32[]{:S(2)}) collective-permute-start(bf16[896,1216]{0,1:T(8,128)(2,1)} %fusion.95), channel_id=1, source_target_pairs={{0,16},{16,0},{1,17},{17,1},{2,18},{18,2},{3,19},{19,3},{4,20},{20... | collective-permute-start | bytes 6537224 | tf_op jit(solution)/shard_map/ppermute | solution.py:111
  1379.0 190.0 %collective-permute-start.34 = (bf16[896,2432]{1,0:T(8,128)(2,1)}, bf16[896,2432]{1,0:T(8,128)(2,1)}, u32[]{:S(2)}, u32[]{:S(2)}) collective-permute-start(bf16[896,2432]{1,0:T(8,128)(2,1)} %convolution_convert_fusion.2), channel_id=1, source_target_pairs={{0,16},{16,0},{1,17},{17,1},{2,18},{18,2},{3,19},{19,3},{4,20},{20... | collective-permute-start | bytes 13074440 | tf_op jit(solution)/shard_map/ppermute | solution.py:111
  1453.0 116.0 %collective-permute-start.43 = (bf16[2,224,1216]{2,1,0:T(8,128)(2,1)}, bf16[2,224,1216]{2,1,0:T(8,128)(2,1)}, u32[]{:S(2)}, u32[]{:S(2)}) collective-permute-start(bf16[2,224,1216]{2,1,0:T(8,128)(2,1)} %get-tuple-element.211), channel_id=1, source_target_pairs={{0,4},{4,0},{8,12},{12,8},{1,5},{5,1},{9,13},{13,9},{2,6},{6,2},{1... | collective-permute-start | bytes 3268616 | tf_op jit(solution)/shard_map/ppermute | solution.py:111
  1484.0 240.3 %all-to-all-start.2 = ((bf16[16,32,1792]{2,1,0:T(8,128)(2,1)}), bf16[16,32,1792]{2,1,0:T(8,128)(2,1)S(1)}, u32[]{:S(2)}, u32[]{:S(2)}) async-start(bf16[16,32,1792]{2,1,0:T(8,128)(2,1)} %bitcast.526), calls=%async_computation.2 | async-start | bytes 3670016 | tf_op jit(solution)/shard_map/all_to_all | solution.py:70
  1498.4 125.0 %collective-permute-start.58 = (bf16[2,896,448]{1,2,0:T(8,128)(2,1)}, bf16[2,896,448]{1,2,0:T(8,128)(2,1)}, u32[]{:S(2)}, u32[]{:S(2)}) collective-permute-start(bf16[2,896,448]{1,2,0:T(8,128)(2,1)} %fusion.227), channel_id=1, source_target_pairs={{0,16},{16,0},{1,17},{17,1},{2,18},{18,2},{3,19},{19,3},{4,20},{20... | collective-permute-start | bytes 4816904 | tf_op jit(solution)/shard_map/ppermute | solution.py:111
  1535.2 105.9 %collective-permute-start.49 = (bf16[1,1792,448]{1,2,0:T(8,128)(2,1)}, bf16[1,1792,448]{1,2,0:T(8,128)(2,1)}, u32[]{:S(2)}, u32[]{:S(2)}) collective-permute-start(bf16[1,1792,448]{1,2,0:T(8,128)(2,1)} %fusion.127), channel_id=1, source_target_pairs={{0,2},{2,0},{1,3},{3,1},{4,6},{6,4},{5,7},{7,5},{8,10},{10,8},{9,1... | collective-permute-start | bytes 4816904 | tf_op jit(solution)/shard_map/ppermute | solution.py:111
  1586.5 86.7 %collective-permute-start.45 = (bf16[2,896,448]{1,2,0:T(8,128)(2,1)}, bf16[2,896,448]{1,2,0:T(8,128)(2,1)}, u32[]{:S(2)}, u32[]{:S(2)}) collective-permute-start(bf16[2,896,448]{1,2,0:T(8,128)(2,1)} %fusion.224), channel_id=1, source_target_pairs={{0,16},{16,0},{1,17},{17,1},{2,18},{18,2},{3,19},{19,3},{4,20},{20... | collective-permute-start | bytes 4816904 | tf_op jit(solution)/shard_map/ppermute | solution.py:111
  1619.9 97.0 %collective-permute-start.62 = (bf16[2,224,2432]{2,1,0:T(8,128)(2,1)}, bf16[2,224,2432]{2,1,0:T(8,128)(2,1)}, u32[]{:S(2)}, u32[]{:S(2)}) collective-permute-start(bf16[2,224,2432]{2,1,0:T(8,128)(2,1)} %dynamic-slice_bitcast_fusion), channel_id=1, source_target_pairs={{0,4},{4,0},{8,12},{12,8},{1,5},{5,1},{9,13},{13,9},{2,6},{6,2},{1... | collective-permute-start | bytes 6537224 | tf_op jit(solution)/shard_map/ppermute | solution.py:111
  1637.9 83.1 %collective-permute-start.59 = (bf16[4,224,448]{2,1,0:T(8,128)(2,1)}, bf16[4,224,448]{2,1,0:T(8,128)(2,1)}, u32[]{:S(2)}, u32[]{:S(2)}) collective-permute-start(bf16[4,224,448]{2,1,0:T(8,128)(2,1)} %bitcast.584), channel_id=1, source_target_pairs={{0,2},{2,0},{1,3},{3,1},{4,6},{6,4},{5,7},{7,5},{8,10},{10,8},{9,1... | collective-permute-start | bytes 2408456 | tf_op jit(solution)/shard_map/ppermute | solution.py:111
  1720.9 120.6 %collective-permute-start.63 = (bf16[224,2432]{1,0:T(8,128)(2,1)}, bf16[224,2432]{1,0:T(8,128)(2,1)}, u32[]{:S(2)}, u32[]{:S(2)}) collective-permute-start(bf16[224,2432]{1,0:T(8,128)(2,1)} %dynamic-slice_bitcast_fusion.4), channel_id=1, source_target_pairs={{0,8},{4,12},{8,0},{12,4},{1,9},{5,13},{9,1},{13,5},{2,10},{6,14},... | collective-permute-start | bytes 3268616 | tf_op jit(solution)/shard_map/ppermute | solution.py:111
  1724.4 127.5 %all-to-all-start.3 = ((bf16[16,32,1792]{2,1,0:T(8,128)(2,1)}), bf16[16,32,1792]{2,1,0:T(8,128)(2,1)}, u32[]{:S(2)}, u32[]{:S(2)}) async-start(bf16[16,32,1792]{2,1,0:T(8,128)(2,1)} %bitcast.527), calls=%async_computation.3 | async-start | bytes 3670016 | tf_op jit(solution)/shard_map/all_to_all | solution.py:70
  1734.5 72.3 %collective-permute-start.47 = (bf16[2,224,448]{2,1,0:T(8,128)(2,1)S(1)}, bf16[2,224,448]{2,1,0:T(8,128)(2,1)S(1)}, u32[]{:S(2)}, u32[]{:S(2)}) collective-permute-start(bf16[2,224,448]{2,1,0:T(8,128)(2,1)S(1)} %dynamic-slice_bitcast_fusion.9), channel_id=1, source_target_pairs={{0,4},{4,0},{8,12},{12,8},{1,5},{5,1},{9,13},{13,9},{2,6},{6,2},{1... | collective-permute-start | bytes 1204232 | tf_op jit(solution)/shard_map/ppermute | solution.py:111
  1756.8 72.2 %collective-permute-start.61 = (bf16[224,448]{1,0:T(8,128)(2,1)S(1)}, bf16[224,448]{1,0:T(8,128)(2,1)S(1)}, u32[]{:S(2)}, u32[]{:S(2)}) collective-permute-start(bf16[224,448]{1,0:T(8,128)(2,1)S(1)} %dynamic-slice_bitcast_fusion.12), channel_id=1, source_target_pairs={{0,8},{4,12},{8,0},{12,4},{1,9},{5,13},{9,1},{13,5},{2,10},{6,14},... | collective-permute-start | bytes 602120 | tf_op jit(solution)/shard_map/ppermute | solution.py:111
  (214 other events, 4450.2 us)
Sparse Core Ops, SparseCore 0:
  11.3 160.8 all-gather.4
  175.8 222.4 all-gather.6
  401.6 139.6 all-gather.8
  544.8 202.4 all-gather.10
  1299.5 305.4 reduce-scatter.1

commit v2 on v1

--- a/solution.py
+++ b/solution.py
@@ -367,22 +367,22 @@
 
 def pair_grad(rows, first, grad, second):
     count, width = rows.shape
-    a, b = first.shape[1], second.shape[1]
+    groups, a, b = first.shape[0], first.shape[2], second.shape[2]
     block = 256
     return pl.pallas_call(
         pair_grad_kernel,
-        grid=(width // block,),
+        grid=(groups, width // block),
         in_specs=[
-            pl.BlockSpec((count, block), lambda i: (0, i)),
-            pl.BlockSpec((count, a), lambda i: (0, 0)),
-            pl.BlockSpec((count, block), lambda i: (0, i)),
-            pl.BlockSpec((count, b), lambda i: (0, 0)),
+            pl.BlockSpec((count, block), lambda y, i: (0, i)),
+            pl.BlockSpec((None, count, a), lambda y, i: (y, 0, 0)),
+            pl.BlockSpec((count, block), lambda y, i: (0, i)),
+            pl.BlockSpec((None, count, b), lambda y, i: (y, 0, 0)),
         ],
-        out_specs=pl.BlockSpec((block, a + b), lambda i: (i, 0)),
-        out_shape=jax.ShapeDtypeStruct((width, a + b), bf16),
+        out_specs=pl.BlockSpec((None, block, a + b), lambda y, i: (y, i, 0)),
+        out_shape=jax.ShapeDtypeStruct((groups, width, a + b), bf16),
         cost_estimate=pl.CostEstimate(
-            flops=2 * count * width * (a + b),
-            bytes_accessed=2 * (2 * count * width + (count + width) * (a + b)),
+            flops=2 * groups * count * width * (a + b),
+            bytes_accessed=2 * groups * (2 * count * width + (count + width) * (a + b)),
             transcendentals=0,
         ),
         compiler_params=pltpu.CompilerParams(vmem_limit_bytes=56 * 2**20),
@@ -581,21 +581,22 @@
     hid_three, z_three = ffn_forward(normed_three, w_f2_in)
 
     grad_z = ffn_backward(grad_out, w_f2_out, z_three)
-    g_f2 = pair_grad(normed_three, grad_z, grad_out, hid_three)
+    g_f2 = pair_grad(normed_three, grad_z[None], grad_out, hid_three[None])[0]
     terms, g_f2 = collect_wide(grad_z, w_f2_in, g_f2)
     step, gain_three = norm_back(stream_three, terms, gains[3])
     upstream = upstream + step
     grad_out = grad_rows(upstream)
     grad_z = attn_backward(grad_out, w_a_out, stored_two, heads, slot_rows)
     g_f2 = scatter_grad(g_f2, LAYER_AXES)
-    g_f2_in, g_f2_out = g_f2[:, :ffn_width], g_f2[:, ffn_width:]
-    g_a_out = reduce_grad(grad_out, hid_two, "fsdp")
-    g_a_in = reduce_grad(normed_two, grad_z, "y")
+    wide_z = jnp.pad(grad_z, ((0, 0), (0, 0), (0, attn_start - attn_width)))
+    g_a = pair_grad(normed_two, wide_z, grad_out, hid_two)
     step, gain_two = norm_back(stream_two, rows.collect(grad_z, w_a_in), gains[2])
     upstream = upstream + step
     upstream, hid_three = tie(upstream, hid_three)
     last_terms = products_wide(hid_three, w_f2_out)
-    grad_out, *last_terms = grad_rows(upstream, spread_wide, *last_terms)
+    grad_out, g_a, *last_terms = grad_rows(upstream, spread_wide, g_a, *last_terms)
+    g_a = scatter_grad(g_a, WEIGHT_AXES)
+    g_a_in, g_a_out = g_a[:, :attn_width], g_a[:, attn_start:]
     out_arrived = reduce_start(grad_out, hid_one)
     grad_z = ffn_backward(grad_out, w_f1_out, z_one)
     in_arrived = reduce_start(normed_one, grad_z)
@@ -614,9 +615,8 @@
         grad_out, w_c_out, kernel, stored_zero, slot_rows
     )
     g_c_gate = reduce_grad(normed_zero, grad_gate, "y")
-    grad_signal, in_arrived, g_a_in, g_a_out, *out_parts = tie(
-        grad_signal, in_arrived, g_a_in, g_a_out, *out_parts
-    )
+    grad_signal, in_arrived, g_f2, *out_parts = tie(grad_signal, in_arrived, g_f2, *out_parts)
+    g_f2_in, g_f2_out = g_f2[:, :ffn_width], g_f2[:, ffn_width:]
     g_f1_out = halve_rest(*out_parts, "ctx").astype(f32)
     g_f1_in = halve_rest(*reduce_middle(normed_one, grad_z, in_arrived), "ctx").astype(f32)
     g_c_signal = reduce_grad(normed_zero, grad_signal, "fsdp")

time: 1890 us -> 1870 us (0.989)
  waiting for transfers between devices: 864 us -> 891 us
  starting transfers between devices: 99.4 us -> 77.5 us
  matrix products: 387 us -> 367 us
  Pallas kernels: 75.8 us -> 95.5 us
    ppermute x5, waiting for transfers between devices: 4.05 us -> 29.5 us  [sum_everywhere(): lax.ppermute(value, axis, [(i, i ^ step) for i in range(size)])]
    ppermute x34 -> x26, starting transfers between devices: 53.3 us -> 30.8 us  [swap(): lax.ppermute(value, axis, [(i, i ^ step) for i in range(lax.axis_size(axi...]
    dot_general x10 -> x6, matrix products: 50.8 us -> 31.3 us  [weight_grad(): return jnp.einsum('rd,yrk->ydk', rows, value, preferred_element_type=f32)]
    pallas_call x1 -> x2, Pallas kernels: 37.4 us -> 56.9 us  [pair_grad(): pl.pallas_call(pair_grad_kernel, grid=(groups, width // block), in_specs=...]
    reduce_scatter x1, waiting for transfers between devices: 0.01 us -> 19.4 us  [scatter_grad(): lax.psum_scatter(flat, axes, scatter_dimension=0, tiled=True).astype(f32)]
    ppermute x34 -> x26, waiting for transfers between devices: 410 us -> 403 us  [swap(): lax.ppermute(value, axis, [(i, i ^ step) for i in range(lax.axis_size(axi...]
    unnamed x339 -> x332, local copies, waits for them, and re-layouts: 42.1 us -> 46.1 us
  transfers between devices with their start and end apart: 74 -> 67, of which waited for: 38 -> 34; matrix products, arithmetic and copies ran while one was open for 33% -> 30% of each run, Pallas kernels for 3% -> 4%
where the time goes in v2:
time: 1870 us; the launch traced here: 1860 us
  waiting for transfers between devices  891 us (48%)
  matrix products  367 us (20%)
  local copies, waits for them, and re-layouts  249 us (13%)
  other arithmetic  163 us (9%)
  Pallas kernels  95.5 us (5%)
  starting transfers between devices  77.5 us (4%)
  between operations  19.6 us (1%)
    ppermute x26, waiting for transfers between devices, swap(): lax.ppermute(value, axis, [(i, i ^ step) for i in range(lax.axis_size(axi...  403 us
    all_gather x2, waiting for transfers between devices, gather_weight(): whole = lax.all_gather(weight, WEIGHT_AXES, axis=0, tiled=True)  163 us
    ppermute x6, waiting for transfers between devices, from_behind(): return lax.ppermute(block, axis, route)  140 us
    dot_general x8, matrix products, part(): return jnp.einsum('rk,dk->rd', flat, weight, preferred_element_type=f32)  89.3 us
    all_to_all x4, waiting for transfers between devices, regroup(): lax.all_to_all(rows[order], ('ctx', 'y', 'core'), split_axis=0, concat_ax...  57.2 us
    pallas_call x2, Pallas kernels, pair_grad(): pl.pallas_call(pair_grad_kernel, grid=(groups, width // block), in_specs=...  56.9 us
    all_gather x2, waiting for transfers between devices, gather_slice(): return lax.all_gather(weight, LAYER_AXES, axis=0, tiled=True)  53.4 us
    dot_general x2, matrix products, slice_project(): return jnp.einsum('rd,dk->rk', rows, weight, preferred_element_type=f32)  48.6 us
  transfers between devices with their start and end apart: 67, of which 34 were waited for; matrix products, arithmetic and copies ran while one was open for 30% of the time, Pallas kernels for 4%

profile of v2, /device:TPU:0, one launch (start us, length us, event | category | flops | bytes accessed | tf_op | source)
XLA Modules:
  0.0 1862.2 jit_solution(1961916102082955595)
XLA Ops:
  30.3 57.2 %all-to-all-done = bf16[16,32,1792]{2,1,0:T(8,128)(2,1)S(1)} async-done(((bf16[16,32,1792]{2,1,0:T(8,128)(2,1)}), bf16[16,32,1792]{2,1,0:T(8,128)(2,1)S(1)}, u32[]{:S(2)}, u32[]{:S(2)}) %all-to-all-start) | async-done | bytes 1835040 | tf_op jit(solution)/shard_map/all_to_all | solution.py:70
  92.6 79.6 %all-gather.5.cloned.1.call-done = bf16[3584,1344]{1,0:T(8,128)(2,1)} async-done(((bf16[224,1344]{1,0:T(8,128)(2,1)}), bf16[3584,1344]{1,0:T(8,128)(2,1)}) %all-gather.5.cloned.1.call-update) | async-done | bytes 9633808 | tf_op jit(solution)/shard_map/all_gather | solution.py:81
  215.9 32.5 %collective-permute-done.1 = bf16[2,2,2,448]{3,2,1,0:T(2,128)(2,1)S(1)} collective-permute-done((bf16[2,2,2,448]{3,2,1,0:T(2,128)(2,1)S(1)}, bf16[2,2,2,448]{3,2,1,0:T(2,128)(2,1)S(1)}, u32[]{:S(2)}, u32[]{:S(2)}) %collective-permute-start.1) | collective-permute-done | bytes 7200 | tf_op jit(solution)/shard_map/ppermute | solution.py:23
  275.0 33.3 %collective-permute-done.5 = bf16[1,512,1792]{2,1,0:T(8,128)(2,1)S(1)} collective-permute-done((bf16[1,512,1792]{2,1,0:T(8,128)(2,1)S(1)}, bf16[1,512,1792]{2,1,0:T(8,128)(2,1)S(1)}, u32[]{:S(2)}, u32[]{:S(2)}) %collective-permute-start.5) | collective-permute-done | bytes 1835040 | tf_op jit(solution)/shard_map/ppermute | solution.py:111
  311.5 36.2 %collective-permute-done.3 = bf16[1,512,1792]{2,1,0:T(8,128)(2,1)S(1)} collective-permute-done((bf16[1,512,1792]{2,1,0:T(8,128)(2,1)S(1)}, bf16[1,512,1792]{2,1,0:T(8,128)(2,1)S(1)}, u32[]{:S(2)}, u32[]{:S(2)}) %collective-permute-start.3) | collective-permute-done | bytes 1835040 | tf_op jit(solution)/shard_map/ppermute | solution.py:111
  351.4 46.7 %all-gather.7.cloned.1.call-done = bf16[1792,3648]{1,0:T(8,128)(2,1)} async-done(((bf16[224,3648]{1,0:T(8,128)(2,1)}), bf16[1792,3648]{1,0:T(8,128)(2,1)}) %all-gather.7.cloned.1.call-update) | async-done | bytes 13074448 | tf_op jit(solution)/shard_map/all_gather | solution.py:86
  411.2 23.3 %convolution_convert_fusion.1.z_ref = bf16[2048,2432]{1,0:T(8,128)(2,1)S(1)} fusion(bf16[2048,1792]{1,0:T(8,128)(2,1)S(1)} %bitcast.468, bf16[1792,3648]{1,0:T(8,128)(2,1)} %all-gather.7.cloned.1.call-done), kind=kOutput, calls=%fused_computation.22 | convolution fusion | flops 17855938560 | bytes 26017792 | tf_op jit(solution)/shard_map/rd,dk->rk/dot_general | solution.py:262
  458.2 83.1 %all-gather.9.cloned.1.call-done = bf16[3584,1088]{1,0:T(8,128)(2,1)} async-done(((bf16[224,1088]{1,0:T(8,128)(2,1)}), bf16[3584,1088]{1,0:T(8,128)(2,1)}) %all-gather.9.cloned.1.call-update) | async-done | bytes 7798800 | tf_op jit(solution)/shard_map/all_gather | solution.py:81
  593.7 26.6 %collective-permute-done.11 = bf16[2,2,4,153,113]{4,2,3,1,0:T(4,128)(2,1)S(1)} collective-permute-done((bf16[2,2,4,153,113]{4,2,3,1,0:T(4,128)(2,1)S(1)}, bf16[2,2,4,153,113]{4,2,3,1,0:T(4,128)(2,1)S(1)}, u32[]{:S(2)}, u32[]{:S(2)}) %collective-permute-start.11) | collective-permute-done | bytes 553280 | tf_op jit(solution)/shard_map/ppermute | solution.py:23
  628.2 25.3 %collective-permute-done.12 = bf16[2,2,4,153,113]{4,2,3,1,0:T(4,128)(2,1)S(1)} collective-permute-done((bf16[2,2,4,153,113]{4,2,3,1,0:T(4,128)(2,1)S(1)}, bf16[2,2,4,153,113]{4,2,3,1,0:T(4,128)(2,1)S(1)}, u32[]{:S(2)}, u32[]{:S(2)}) %collective-permute-start.12) | collective-permute-done | bytes 553280 | tf_op jit(solution)/shard_map/ppermute | solution.py:23
  689.7 40.6 %collective-permute-done.14 = bf16[1,512,1792]{2,1,0:T(8,128)(2,1)S(1)} collective-permute-done((bf16[1,512,1792]{2,1,0:T(8,128)(2,1)S(1)}, bf16[1,512,1792]{2,1,0:T(8,128)(2,1)S(1)}, u32[]{:S(2)}, u32[]{:S(2)}) %collective-permute-start.14) | collective-permute-done | bytes 1835040 | tf_op jit(solution)/shard_map/ppermute | solution.py:111
  747.2 25.3 %convolution_convert_fusion.z_ref = bf16[2048,2432]{1,0:T(8,128)(2,1)} fusion(bf16[2048,1792]{1,0:T(8,128)(2,1)} %bitcast.478, bf16[1792,3648]{1,0:T(8,128)(2,1)} %all-gather.11.cloned.1.call-done), kind=kOutput, calls=%fused_computation.21 | convolution fusion | flops 17855938560 | bytes 26017792 | tf_op jit(solution)/shard_map/rd,dk->rk/dot_general | solution.py:262
  850.8 37.4 %shard_map.275 = bf16[1,1792,3648]{2,1,0:T(8,128)(2,1)} custom-call(bf16[2048,1792]{1,0:T(8,128)(2,1)} %bitcast.479, bf16[1,2048,2432]{2,1,0:T(8,128)(2,1)} %bitcast.461, bf16[2048,1792]{1,0:T(8,128)(2,1)} %bitcast.477, bf16[1,2048,1216]{2,1,0:T(8,128)(2,1)} %fusion.387.second_ref), custom_call_target="tpu_custom_call" | custom-call | flops 26776436736 | bytes 42696704 | tf_op jit(solution)/shard_map/pallas_call | solution.py:372
  1012.5 37.6 %collective-permute-done.21 = bf16[2,2,4,153,113]{4,2,3,1,0:T(4,128)(2,1)S(1)} collective-permute-done((bf16[2,2,4,153,113]{4,2,3,1,0:T(4,128)(2,1)}, bf16[2,2,4,153,113]{4,2,3,1,0:T(4,128)(2,1)S(1)}, u32[]{:S(2)}, u32[]{:S(2)}) %collective-permute-start.21) | collective-permute-done | bytes 553280 | tf_op jit(solution)/shard_map/ppermute | solution.py:23
  1106.7 19.5 %shard_map.276 = bf16[2,1792,1088]{2,1,0:T(8,128)(2,1)} custom-call(bf16[1024,1792]{1,0:T(8,128)(2,1)} %pad_maximum_fusion.8.rows_ref, bf16[2,1024,640]{2,1,0:T(8,128)(2,1)} %pad.5.first_ref, bf16[1024,1792]{1,0:T(8,128)(2,1)} %copy-done.58, bf16[2,1024,448]{2,1,0:T(8,128)(2,1)} %copy.357.second_ref), custom_call_target="tpu_custom_call" | custom-call | flops 7985954816 | bytes 26935296 | tf_op jit(solution)/shard_map/pallas_call | solution.py:372
  1159.1 19.4 %shard_map.277 = bf16[2048,2432]{1,0:T(8,128)(2,1)} custom-call(bf16[2048,1792]{1,0:T(8,128)(2,1)} %bitcast.471, bf16[1792,1216]{1,0:T(8,128)(2,1)} %slice.432.weight_ref, bf16[2048,2432]{1,0:T(8,128)(2,1)} %copy-done.38), custom_call_target="tpu_custom_call" | custom-call | flops 8925478912 | bytes 31621120 | tf_op jit(solution)/shard_map/pallas_call | solution.py:338
  1248.0 22.6 %collective-permute-done.27 = bf16[512,1792]{1,0:T(8,128)(2,1)S(1)} collective-permute-done((bf16[512,1792]{1,0:T(8,128)(2,1)}, bf16[512,1792]{1,0:T(8,128)(2,1)S(1)}, u32[]{:S(2)}, u32[]{:S(2)}) %collective-permute-start.27) | collective-permute-done | bytes 1835040 | tf_op jit(solution)/shard_map/ppermute | solution.py:111
  1377.2 93.6 %collective-permute-done.50 = bf16[2,896,448]{1,2,0:T(8,128)(2,1)} collective-permute-done((bf16[2,896,448]{1,2,0:T(8,128)(2,1)}, bf16[2,896,448]{1,2,0:T(8,128)(2,1)}, u32[]{:S(2)}, u32[]{:S(2)}) %collective-permute-start.50) | collective-permute-done | bytes 1605664 | tf_op jit(solution)/shard_map/ppermute | solution.py:111
  1514.8 30.8 %collective-permute-done.42 = bf16[4,224,448]{2,1,0:T(8,128)(2,1)} collective-permute-done((bf16[4,224,448]{2,1,0:T(8,128)(2,1)}, bf16[4,224,448]{2,1,0:T(8,128)(2,1)}, u32[]{:S(2)}, u32[]{:S(2)}) %collective-permute-start.42) | collective-permute-done | bytes 802848 | tf_op jit(solution)/shard_map/ppermute | solution.py:111
  1550.7 24.5 %collective-permute-done.43 = bf16[2,224,448]{2,1,0:T(8,128)(2,1)S(1)} collective-permute-done((bf16[2,224,448]{2,1,0:T(8,128)(2,1)S(1)}, bf16[2,224,448]{2,1,0:T(8,128)(2,1)S(1)}, u32[]{:S(2)}, u32[]{:S(2)}) %collective-permute-start.43) | collective-permute-done | bytes 401440 | tf_op jit(solution)/shard_map/ppermute | solution.py:111
  1682.9 22.0 %collective-permute-done.37 = bf16[2,896,448]{1,2,0:T(8,128)(2,1)} collective-permute-done((bf16[2,896,448]{1,2,0:T(8,128)(2,1)}, bf16[2,896,448]{1,2,0:T(8,128)(2,1)}, u32[]{:S(2)}, u32[]{:S(2)}) %collective-permute-start.37) | collective-permute-done | bytes 1605664 | tf_op jit(solution)/shard_map/ppermute | solution.py:111
  1748.1 32.8 %collective-permute-done.39 = bf16[2,224,448]{2,1,0:T(8,128)(2,1)S(1)} collective-permute-done((bf16[2,224,448]{2,1,0:T(8,128)(2,1)S(1)}, bf16[2,224,448]{2,1,0:T(8,128)(2,1)S(1)}, u32[]{:S(2)}, u32[]{:S(2)}) %collective-permute-start.39) | collective-permute-done | bytes 401440 | tf_op jit(solution)/shard_map/ppermute | solution.py:111
  1787.5 25.6 %collective-permute-done.49 = f32[7,1792]{1,0:T(8,128)S(1)} collective-permute-done((f32[7,1792]{1,0:T(8,128)S(1)}, f32[7,1792]{1,0:T(8,128)S(1)}, u32[]{:S(2)}, u32[]{:S(2)}) %collective-permute-start.49) | collective-permute-done | bytes 50208 | tf_op jit(solution)/shard_map/ppermute | solution.py:43
  1814.3 26.5 %collective-permute-done.40 = bf16[224,448]{1,0:T(8,128)(2,1)S(1)} collective-permute-done((bf16[224,448]{1,0:T(8,128)(2,1)S(1)}, bf16[224,448]{1,0:T(8,128)(2,1)S(1)}, u32[]{:S(2)}, u32[]{:S(2)}) %collective-permute-start.40) | collective-permute-done | bytes 200736 | tf_op jit(solution)/shard_map/ppermute | solution.py:111
  (745 shorter events, 940.7 us)
Async XLA Ops:
  7.2 165.0 %all-gather.5.cloned.1.call-start = ((), (), s32[]{:S(2)}) async-start(), calls=%async_computation.6 | async-start | bytes 10723328 | tf_op jit(solution)/shard_map/all_gather | solution.py:81
  21.0 66.5 %all-to-all-start = ((bf16[16,32,1792]{2,1,0:T(8,128)(2,1)}), bf16[16,32,1792]{2,1,0:T(8,128)(2,1)S(1)}, u32[]{:S(2)}, u32[]{:S(2)}) async-start(bf16[16,32,1792]{2,1,0:T(8,128)(2,1)} %bitcast.467), calls=%async_computation | async-start | bytes 3670016 | tf_op jit(solution)/shard_map/all_to_all | solution.py:70
  28.3 369.8 %all-gather.7.cloned.1.call-start = ((), (), s32[]{:S(2)}) async-start(), calls=%async_computation.7 | async-start | bytes 14966784 | tf_op jit(solution)/shard_map/all_gather | solution.py:86
  184.0 74.7 %all-to-all-start.1 = ((bf16[16,32,1792]{2,1,0:T(8,128)(2,1)}), bf16[16,32,1792]{2,1,0:T(8,128)(2,1)S(1)}, u32[]{:S(2)}, u32[]{:S(2)}) async-start(bf16[16,32,1792]{2,1,0:T(8,128)(2,1)} %bitcast.465), calls=%async_computation.1 | async-start | bytes 3670016 | tf_op jit(solution)/shard_map/all_to_all | solution.py:70
  187.9 353.4 %all-gather.9.cloned.1.call-start = ((), (), s32[]{:S(2)}) async-start(), calls=%async_computation.8 | async-start | bytes 8773632 | tf_op jit(solution)/shard_map/all_gather | solution.py:81
  274.4 73.2 %collective-permute-start.3 = (bf16[1,512,1792]{2,1,0:T(8,128)(2,1)S(1)}, bf16[1,512,1792]{2,1,0:T(8,128)(2,1)S(1)}, u32[]{:S(2)}, u32[]{:S(2)}) collective-permute-start(bf16[1,512,1792]{2,1,0:T(8,128)(2,1)S(1)} %fusion.168), channel_id=1, source_target_pairs={{0,2},{2,0},{1,3},{3,1},{4,6},{6,4},{5,7},{7,5},{8,10},{10,8},{9,1... | collective-permute-start | bytes 5505032 | tf_op jit(solution)/shard_map/ppermute | solution.py:111
  310.9 90.5 %collective-permute-start.6 = (bf16[2,512,1792]{2,1,0:T(8,128)(2,1)}, bf16[2,512,1792]{2,1,0:T(8,128)(2,1)}, u32[]{:S(2)}, u32[]{:S(2)}) collective-permute-start(bf16[2,512,1792]{2,1,0:T(8,128)(2,1)} %pad_maximum_fusion.7), channel_id=1, source_target_pairs={{0,1},{1,0},{2,3},{3,2},{4,5},{5,4},{6,7},{7,6},{8,9},{9,8},{10,11... | collective-permute-start | bytes 11010056 | tf_op jit(solution)/shard_map/ppermute | solution.py:77
  400.8 346.4 %all-gather.11.cloned.1.call-start = ((), (), s32[]{:S(2)}) async-start(), calls=%async_computation.9 | async-start | bytes 14966784 | tf_op jit(solution)/shard_map/all_gather | solution.py:86
  455.8 97.5 %collective-permute-start.8 = (bf16[512,1792]{1,0:T(8,128)(2,1)}, bf16[512,1792]{1,0:T(8,128)(2,1)}, u32[]{:S(2)}, u32[]{:S(2)}) collective-permute-start(bf16[512,1792]{1,0:T(8,128)(2,1)} %fusion.173), channel_id=1, source_target_pairs={{0,2},{2,0},{1,3},{3,1},{4,6},{6,4},{5,7},{7,5},{8,10},{10,8},{9,1... | collective-permute-start | bytes 5505032 | tf_op jit(solution)/shard_map/ppermute | solution.py:111
  544.6 1061.5 %reduce-scatter.7.cloned.1.call-start = ((), (), s32[]{:S(2)}) async-start(), calls=%async_computation.11 | async-start | bytes 8773632
  1142.4 486.2 %reduce-scatter.5.cloned.1.call-start = ((), (), s32[]{:S(2)}) async-start(), calls=%async_computation.10 | async-start | bytes 14966784 | tf_op jit(solution)/shard_map/reduce_scatter | solution.py:91
  1246.5 60.0 %collective-permute-start.29 = (bf16[896,1216]{0,1:T(8,128)(2,1)}, bf16[896,1216]{0,1:T(8,128)(2,1)}, u32[]{:S(2)}, u32[]{:S(2)}) collective-permute-start(bf16[896,1216]{0,1:T(8,128)(2,1)} %fusion.94), channel_id=1, source_target_pairs={{0,16},{16,0},{1,17},{17,1},{2,18},{18,2},{3,19},{19,3},{4,20},{20... | collective-permute-start | bytes 6537224 | tf_op jit(solution)/shard_map/ppermute | solution.py:111
  1284.5 345.9 %collective-permute-start.34 = (bf16[896,2432]{1,0:T(8,128)(2,1)}, bf16[896,2432]{1,0:T(8,128)(2,1)}, u32[]{:S(2)}, u32[]{:S(2)}) collective-permute-start(bf16[896,2432]{1,0:T(8,128)(2,1)} %convolution_convert_fusion.2), channel_id=1, source_target_pairs={{0,16},{16,0},{1,17},{17,1},{2,18},{18,2},{3,19},{19,3},{4,20},{20... | collective-permute-start | bytes 13074440 | tf_op jit(solution)/shard_map/ppermute | solution.py:111
  1321.9 308.6 %collective-permute-start.35 = (bf16[2,224,1216]{2,1,0:T(8,128)(2,1)}, bf16[2,224,1216]{2,1,0:T(8,128)(2,1)}, u32[]{:S(2)}, u32[]{:S(2)}) collective-permute-start(bf16[2,224,1216]{2,1,0:T(8,128)(2,1)} %get-tuple-element.199), channel_id=1, source_target_pairs={{0,4},{4,0},{8,12},{12,8},{1,5},{5,1},{9,13},{13,9},{2,6},{6,2},{1... | collective-permute-start | bytes 3268616 | tf_op jit(solution)/shard_map/ppermute | solution.py:111
  1330.3 140.5 %collective-permute-start.50 = (bf16[2,896,448]{1,2,0:T(8,128)(2,1)}, bf16[2,896,448]{1,2,0:T(8,128)(2,1)}, u32[]{:S(2)}, u32[]{:S(2)}) collective-permute-start(bf16[2,896,448]{1,2,0:T(8,128)(2,1)} %fusion.209), channel_id=1, source_target_pairs={{0,16},{16,0},{1,17},{17,1},{2,18},{18,2},{3,19},{19,3},{4,20},{20... | collective-permute-start | bytes 4816904 | tf_op jit(solution)/shard_map/ppermute | solution.py:111
  1363.8 124.9 %collective-permute-start.41 = (bf16[1,1792,448]{1,2,0:T(8,128)(2,1)}, bf16[1,1792,448]{1,2,0:T(8,128)(2,1)}, u32[]{:S(2)}, u32[]{:S(2)}) collective-permute-start(bf16[1,1792,448]{1,2,0:T(8,128)(2,1)} %fusion.124), channel_id=1, source_target_pairs={{0,2},{2,0},{1,3},{3,1},{4,6},{6,4},{5,7},{7,5},{8,10},{10,8},{9,1... | collective-permute-start | bytes 4816904 | tf_op jit(solution)/shard_map/ppermute | solution.py:111
  1370.7 232.3 %all-to-all-start.2 = ((bf16[16,32,1792]{2,1,0:T(8,128)(2,1)}), bf16[16,32,1792]{2,1,0:T(8,128)(2,1)S(1)}, u32[]{:S(2)}, u32[]{:S(2)}) async-start(bf16[16,32,1792]{2,1,0:T(8,128)(2,1)} %bitcast.464), calls=%async_computation.2 | async-start | bytes 3670016 | tf_op jit(solution)/shard_map/all_to_all | solution.py:70
  1375.9 171.7 %collective-permute-start.33 = (f32[2,2,2,448]{3,2,1,0:T(2,128)S(1)}, f32[2,2,2,448]{3,2,1,0:T(2,128)S(1)}, u32[]{:S(2)}, u32[]{:S(2)}) collective-permute-start(f32[2,2,2,448]{3,2,1,0:T(2,128)S(1)} %slice.477), channel_id=1, source_target_pairs={{4,0},{8,4},{12,8},{5,1},{9,5},{13,9},{6,2},{10,6},{14,10},{7,3},{... | collective-permute-start | bytes 43016 | tf_op jit(solution)/shard_map/ppermute | solution.py:23
  1655.4 130.0 %collective-permute-start.56 = (bf16[224,1216]{1,0:T(8,128)(2,1)}, bf16[224,1216]{1,0:T(8,128)(2,1)}, u32[]{:S(2)}, u32[]{:S(2)}) collective-permute-start(bf16[224,1216]{1,0:T(8,128)(2,1)} %dynamic-slice_bitcast_fusion.4), channel_id=1, source_target_pairs={{0,8},{4,12},{8,0},{12,4},{1,9},{5,13},{9,1},{13,5},{2,10},{6,14},... | collective-permute-start | bytes 1634312 | tf_op jit(solution)/shard_map/ppermute | solution.py:111
  1668.7 75.8 %collective-permute-start.54 = (bf16[2,224,2432]{2,1,0:T(8,128)(2,1)}, bf16[2,224,2432]{2,1,0:T(8,128)(2,1)}, u32[]{:S(2)}, u32[]{:S(2)}) collective-permute-start(bf16[2,224,2432]{2,1,0:T(8,128)(2,1)} %dynamic-slice_bitcast_fusion), channel_id=1, source_target_pairs={{0,4},{4,0},{8,12},{12,8},{1,5},{5,1},{9,13},{13,9},{2,6},{6,2},{1... | collective-permute-start | bytes 6537224 | tf_op jit(solution)/shard_map/ppermute | solution.py:111
  1733.7 114.9 %all-to-all-start.3 = ((bf16[16,32,1792]{2,1,0:T(8,128)(2,1)}), bf16[16,32,1792]{2,1,0:T(8,128)(2,1)}, u32[]{:S(2)}, u32[]{:S(2)}) async-start(bf16[16,32,1792]{2,1,0:T(8,128)(2,1)} %bitcast.466), calls=%async_computation.4 | async-start | bytes 3670016 | tf_op jit(solution)/shard_map/all_to_all | solution.py:70
  1738.5 74.6 %collective-permute-start.49 = (f32[7,1792]{1,0:T(8,128)S(1)}, f32[7,1792]{1,0:T(8,128)S(1)}, u32[]{:S(2)}, u32[]{:S(2)}) collective-permute-start(f32[7,1792]{1,0:T(8,128)S(1)} %add.541), channel_id=1, source_target_pairs={{0,8},{4,12},{8,0},{12,4},{1,9},{5,13},{9,1},{13,5},{2,10},{6,14},... | collective-permute-start | bytes 150536 | tf_op jit(solution)/shard_map/ppermute | solution.py:43
  1747.4 95.3 %collective-permute-start.55 = (bf16[224,2432]{1,0:T(8,128)(2,1)S(1)}, bf16[224,2432]{1,0:T(8,128)(2,1)S(1)}, u32[]{:S(2)}, u32[]{:S(2)}) collective-permute-start(bf16[224,2432]{1,0:T(8,128)(2,1)S(1)} %dynamic-slice_bitcast_fusion.3), channel_id=1, source_target_pairs={{0,8},{4,12},{8,0},{12,4},{1,9},{5,13},{9,1},{13,5},{2,10},{6,14},... | collective-permute-start | bytes 3268616 | tf_op jit(solution)/shard_map/ppermute | solution.py:111
  1781.1 59.8 %collective-permute-start.40 = (bf16[224,448]{1,0:T(8,128)(2,1)S(1)}, bf16[224,448]{1,0:T(8,128)(2,1)S(1)}, u32[]{:S(2)}, u32[]{:S(2)}) collective-permute-start(bf16[224,448]{1,0:T(8,128)(2,1)S(1)} %dynamic-slice_bitcast_fusion.10), channel_id=1, source_target_pairs={{0,8},{4,12},{8,0},{12,4},{1,9},{5,13},{9,1},{13,5},{2,10},{6,14},... | collective-permute-start | bytes 602120 | tf_op jit(solution)/shard_map/ppermute | solution.py:111
  (205 other events, 3953.5 us)
Sparse Core Ops, SparseCore 0:
  11.3 160.7 all-gather.4
  175.7 222.3 all-gather.6
  401.5 139.7 all-gather.8
  544.7 202.4 all-gather.10
  1142.6 177.1 reduce-scatter.6
  1323.3 305.3 reduce-scatter.4

commit v3 on v2

--- a/solution.py
+++ b/solution.py
@@ -588,6 +588,7 @@
     grad_out = grad_rows(upstream)
     grad_z = attn_backward(grad_out, w_a_out, stored_two, heads, slot_rows)
     g_f2 = scatter_grad(g_f2, LAYER_AXES)
+    g_f2_in, g_f2_out = g_f2[:, :ffn_width], g_f2[:, ffn_width:]
     wide_z = jnp.pad(grad_z, ((0, 0), (0, 0), (0, attn_start - attn_width)))
     g_a = pair_grad(normed_two, wide_z, grad_out, hid_two)
     step, gain_two = norm_back(stream_two, rows.collect(grad_z, w_a_in), gains[2])
@@ -615,8 +616,7 @@
         grad_out, w_c_out, kernel, stored_zero, slot_rows
     )
     g_c_gate = reduce_grad(normed_zero, grad_gate, "y")
-    grad_signal, in_arrived, g_f2, *out_parts = tie(grad_signal, in_arrived, g_f2, *out_parts)
-    g_f2_in, g_f2_out = g_f2[:, :ffn_width], g_f2[:, ffn_width:]
+    grad_signal, in_arrived, *out_parts = tie(grad_signal, in_arrived, *out_parts)
     g_f1_out = halve_rest(*out_parts, "ctx").astype(f32)
     g_f1_in = halve_rest(*reduce_middle(normed_one, grad_z, in_arrived), "ctx").astype(f32)
     g_c_signal = reduce_grad(normed_zero, grad_signal, "fsdp")

time: 1870 us -> 1780 us (0.952)
  waiting for transfers between devices: 891 us -> 766 us
  starting transfers between devices: 77.5 us -> 107 us
    ppermute x26, waiting for transfers between devices: 403 us -> 287 us  [swap(): lax.ppermute(value, axis, [(i, i ^ step) for i in range(lax.axis_size(axi...]
    ppermute x26, starting transfers between devices: 30.8 us -> 62.2 us  [swap(): lax.ppermute(value, axis, [(i, i ^ step) for i in range(lax.axis_size(axi...]
    reduce_scatter x1, waiting for transfers between devices: 19.4 us -> 0.01 us  [scatter_grad(): lax.psum_scatter(flat, axes, scatter_dimension=0, tiled=True).astype(f32)]
    ppermute x6, waiting for transfers between devices: 140 us -> 159 us  [from_behind(): return lax.ppermute(block, axis, route)]
  transfers between devices with their start and end apart: 67 -> 67, of which waited for: 34 -> 34; matrix products, arithmetic and copies ran while one was open for 30% -> 33% of each run, Pallas kernels for 4% -> 4%
where the time goes in v3:
time: 1780 us; the launch traced here: 1770 us
  waiting for transfers between devices  766 us (43%)
  matrix products  365 us (21%)
  local copies, waits for them, and re-layouts  260 us (15%)
  other arithmetic  160 us (9%)
  starting transfers between devices  107 us (6%)
  Pallas kernels  95.7 us (5%)
  between operations  19.5 us (1%)
    ppermute x26, waiting for transfers between devices, swap(): lax.ppermute(value, axis, [(i, i ^ step) for i in range(lax.axis_size(axi...  287 us
    all_gather x2, waiting for transfers between devices, gather_weight(): whole = lax.all_gather(weight, WEIGHT_AXES, axis=0, tiled=True)  163 us
    ppermute x6, waiting for transfers between devices, from_behind(): return lax.ppermute(block, axis, route)  159 us
    dot_general x8, matrix products, part(): return jnp.einsum('rk,dk->rd', flat, weight, preferred_element_type=f32)  87.7 us
    ppermute x26, starting transfers between devices, swap(): lax.ppermute(value, axis, [(i, i ^ step) for i in range(lax.axis_size(axi...  62.2 us
    all_to_all x4, waiting for transfers between devices, regroup(): lax.all_to_all(rows[order], ('ctx', 'y', 'core'), split_axis=0, concat_ax...  57.2 us
    pallas_call x2, Pallas kernels, pair_grad(): pl.pallas_call(pair_grad_kernel, grid=(groups, width // block), in_specs=...  57.1 us
    all_gather x2, waiting for transfers between devices, gather_slice(): return lax.all_gather(weight, LAYER_AXES, axis=0, tiled=True)  53.5 us
  transfers between devices with their start and end apart: 67, of which 34 were waited for; matrix products, arithmetic and copies ran while one was open for 33% of the time, Pallas kernels for 4%

profile of v3, /device:TPU:0, one launch (start us, length us, event | category | flops | bytes accessed | tf_op | source)
XLA Modules:
  0.0 1772.7 jit_solution(1974119225177441230)
XLA Ops:
  30.3 57.2 %all-to-all-done = bf16[16,32,1792]{2,1,0:T(8,128)(2,1)S(1)} async-done(((bf16[16,32,1792]{2,1,0:T(8,128)(2,1)}), bf16[16,32,1792]{2,1,0:T(8,128)(2,1)S(1)}, u32[]{:S(2)}, u32[]{:S(2)}) %all-to-all-start) | async-done | bytes 1835040 | tf_op jit(solution)/shard_map/all_to_all | solution.py:70
  92.6 79.6 %all-gather.5.cloned.1.call-done = bf16[3584,1344]{1,0:T(8,128)(2,1)} async-done(((bf16[224,1344]{1,0:T(8,128)(2,1)}), bf16[3584,1344]{1,0:T(8,128)(2,1)}) %all-gather.5.cloned.1.call-update) | async-done | bytes 9633808 | tf_op jit(solution)/shard_map/all_gather | solution.py:81
  215.7 32.6 %collective-permute-done.1 = bf16[2,2,2,448]{3,2,1,0:T(2,128)(2,1)S(1)} collective-permute-done((bf16[2,2,2,448]{3,2,1,0:T(2,128)(2,1)S(1)}, bf16[2,2,2,448]{3,2,1,0:T(2,128)(2,1)S(1)}, u32[]{:S(2)}, u32[]{:S(2)}) %collective-permute-start.1) | collective-permute-done | bytes 7200 | tf_op jit(solution)/shard_map/ppermute | solution.py:23
  275.1 33.3 %collective-permute-done.5 = bf16[1,512,1792]{2,1,0:T(8,128)(2,1)S(1)} collective-permute-done((bf16[1,512,1792]{2,1,0:T(8,128)(2,1)S(1)}, bf16[1,512,1792]{2,1,0:T(8,128)(2,1)S(1)}, u32[]{:S(2)}, u32[]{:S(2)}) %collective-permute-start.5) | collective-permute-done | bytes 1835040 | tf_op jit(solution)/shard_map/ppermute | solution.py:111
  311.4 36.3 %collective-permute-done.3 = bf16[1,512,1792]{2,1,0:T(8,128)(2,1)S(1)} collective-permute-done((bf16[1,512,1792]{2,1,0:T(8,128)(2,1)S(1)}, bf16[1,512,1792]{2,1,0:T(8,128)(2,1)S(1)}, u32[]{:S(2)}, u32[]{:S(2)}) %collective-permute-start.3) | collective-permute-done | bytes 1835040 | tf_op jit(solution)/shard_map/ppermute | solution.py:111
  351.4 46.8 %all-gather.7.cloned.1.call-done = bf16[1792,3648]{1,0:T(8,128)(2,1)} async-done(((bf16[224,3648]{1,0:T(8,128)(2,1)}), bf16[1792,3648]{1,0:T(8,128)(2,1)}) %all-gather.7.cloned.1.call-update) | async-done | bytes 13074448 | tf_op jit(solution)/shard_map/all_gather | solution.py:86
  411.3 23.3 %convolution_convert_fusion.1.z_ref = bf16[2048,2432]{1,0:T(8,128)(2,1)S(1)} fusion(bf16[2048,1792]{1,0:T(8,128)(2,1)S(1)} %bitcast.470, bf16[1792,3648]{1,0:T(8,128)(2,1)} %all-gather.7.cloned.1.call-done), kind=kOutput, calls=%fused_computation.22 | convolution fusion | flops 17855938560 | bytes 26017792 | tf_op jit(solution)/shard_map/rd,dk->rk/dot_general | solution.py:262
  458.2 83.1 %all-gather.9.cloned.1.call-done = bf16[3584,1088]{1,0:T(8,128)(2,1)} async-done(((bf16[224,1088]{1,0:T(8,128)(2,1)}), bf16[3584,1088]{1,0:T(8,128)(2,1)}) %all-gather.9.cloned.1.call-update) | async-done | bytes 7798800 | tf_op jit(solution)/shard_map/all_gather | solution.py:81
  593.5 26.8 %collective-permute-done.11 = bf16[2,2,4,153,113]{4,2,3,1,0:T(4,128)(2,1)S(1)} collective-permute-done((bf16[2,2,4,153,113]{4,2,3,1,0:T(4,128)(2,1)S(1)}, bf16[2,2,4,153,113]{4,2,3,1,0:T(4,128)(2,1)S(1)}, u32[]{:S(2)}, u32[]{:S(2)}) %collective-permute-start.11) | collective-permute-done | bytes 553280 | tf_op jit(solution)/shard_map/ppermute | solution.py:23
  628.2 25.3 %collective-permute-done.12 = bf16[2,2,4,153,113]{4,2,3,1,0:T(4,128)(2,1)S(1)} collective-permute-done((bf16[2,2,4,153,113]{4,2,3,1,0:T(4,128)(2,1)S(1)}, bf16[2,2,4,153,113]{4,2,3,1,0:T(4,128)(2,1)S(1)}, u32[]{:S(2)}, u32[]{:S(2)}) %collective-permute-start.12) | collective-permute-done | bytes 553280 | tf_op jit(solution)/shard_map/ppermute | solution.py:23
  689.7 40.6 %collective-permute-done.14 = bf16[1,512,1792]{2,1,0:T(8,128)(2,1)S(1)} collective-permute-done((bf16[1,512,1792]{2,1,0:T(8,128)(2,1)S(1)}, bf16[1,512,1792]{2,1,0:T(8,128)(2,1)S(1)}, u32[]{:S(2)}, u32[]{:S(2)}) %collective-permute-start.14) | collective-permute-done | bytes 1835040 | tf_op jit(solution)/shard_map/ppermute | solution.py:111
  747.2 25.3 %convolution_convert_fusion.z_ref = bf16[2048,2432]{1,0:T(8,128)(2,1)} fusion(bf16[2048,1792]{1,0:T(8,128)(2,1)} %bitcast.482, bf16[1792,3648]{1,0:T(8,128)(2,1)} %all-gather.11.cloned.1.call-done), kind=kOutput, calls=%fused_computation.21 | convolution fusion | flops 17855938560 | bytes 26017792 | tf_op jit(solution)/shard_map/rd,dk->rk/dot_general | solution.py:262
  777.2 19.2 %shard_map.274 = bf16[2048,2432]{1,0:T(8,128)(2,1)} custom-call(bf16[2048,1792]{1,0:T(8,128)(2,1)} %bitcast.480, bf16[1792,1216]{1,0:T(8,128)(2,1)} %slice.451.weight_ref, bf16[2048,2432]{1,0:T(8,128)(2,1)} %convolution_convert_fusion.z_ref), custom_call_target="tpu_custom_call" | custom-call | flops 8925478912 | bytes 31621120 | tf_op jit(solution)/shard_map/pallas_call | solution.py:338
  850.8 37.6 %shard_map.275 = bf16[1,1792,3648]{2,1,0:T(8,128)(2,1)} custom-call(bf16[2048,1792]{1,0:T(8,128)(2,1)} %bitcast.483, bf16[1,2048,2432]{2,1,0:T(8,128)(2,1)} %bitcast.463, bf16[2048,1792]{1,0:T(8,128)(2,1)} %bitcast.481, bf16[1,2048,1216]{2,1,0:T(8,128)(2,1)} %fusion.387.second_ref), custom_call_target="tpu_custom_call" | custom-call | flops 26776436736 | bytes 42696704 | tf_op jit(solution)/shard_map/pallas_call | solution.py:372
  1012.7 37.5 %collective-permute-done.21 = bf16[2,2,4,153,113]{4,2,3,1,0:T(4,128)(2,1)S(1)} collective-permute-done((bf16[2,2,4,153,113]{4,2,3,1,0:T(4,128)(2,1)}, bf16[2,2,4,153,113]{4,2,3,1,0:T(4,128)(2,1)S(1)}, u32[]{:S(2)}, u32[]{:S(2)}) %collective-permute-start.21) | collective-permute-done | bytes 553280 | tf_op jit(solution)/shard_map/ppermute | solution.py:23
  1106.7 19.5 %shard_map.276 = bf16[2,1792,1088]{2,1,0:T(8,128)(2,1)} custom-call(bf16[1024,1792]{1,0:T(8,128)(2,1)} %pad_maximum_fusion.8.rows_ref, bf16[2,1024,640]{2,1,0:T(8,128)(2,1)} %pad.5.first_ref, bf16[1024,1792]{1,0:T(8,128)(2,1)} %copy-done.59, bf16[2,1024,448]{2,1,0:T(8,128)(2,1)} %copy.357.second_ref), custom_call_target="tpu_custom_call" | custom-call | flops 7985954816 | bytes 26935296 | tf_op jit(solution)/shard_map/pallas_call | solution.py:372
  1154.5 19.4 %shard_map.277 = bf16[2048,2432]{1,0:T(8,128)(2,1)} custom-call(bf16[2048,1792]{1,0:T(8,128)(2,1)} %bitcast.475, bf16[1792,1216]{1,0:T(8,128)(2,1)} %slice.432.weight_ref, bf16[2048,2432]{1,0:T(8,128)(2,1)} %copy-done.36), custom_call_target="tpu_custom_call" | custom-call | flops 8925478912 | bytes 31621120 | tf_op jit(solution)/shard_map/pallas_call | solution.py:338
  1243.3 20.9 %collective-permute-done.27 = bf16[512,1792]{1,0:T(8,128)(2,1)S(1)} collective-permute-done((bf16[512,1792]{1,0:T(8,128)(2,1)}, bf16[512,1792]{1,0:T(8,128)(2,1)S(1)}, u32[]{:S(2)}, u32[]{:S(2)}) %collective-permute-start.27) | collective-permute-done | bytes 1835040 | tf_op jit(solution)/shard_map/ppermute | solution.py:111
  1321.3 24.9 %collective-permute-done.31 = bf16[512,1792]{1,0:T(8,128)(2,1)} collective-permute-done((bf16[512,1792]{1,0:T(8,128)(2,1)}, bf16[512,1792]{1,0:T(8,128)(2,1)}, u32[]{:S(2)}, u32[]{:S(2)}) %collective-permute-start.31) | collective-permute-done | bytes 1835040 | tf_op jit(solution)/shard_map/ppermute | solution.py:111
  1425.4 23.7 %collective-permute-start.56 = (bf16[224,1216]{1,0:T(8,128)(2,1)S(1)}, bf16[224,1216]{1,0:T(8,128)(2,1)S(1)}, u32[]{:S(2)}, u32[]{:S(2)}) collective-permute-start(bf16[224,1216]{1,0:T(8,128)(2,1)S(1)} %dynamic-slice_bitcast_fusion.4), channel_id=1, source_target_pairs={{0,8},{4,12},{8,0},{12,4},{1,9},{5,13},{9,1},{13,5},{2,10},{6,14},... | collective-permute-start | bytes 1634312 | tf_op jit(solution)/shard_map/ppermute | solution.py:111
  1479.2 23.5 %collective-permute-done.56 = bf16[224,1216]{1,0:T(8,128)(2,1)S(1)} collective-permute-done((bf16[224,1216]{1,0:T(8,128)(2,1)S(1)}, bf16[224,1216]{1,0:T(8,128)(2,1)S(1)}, u32[]{:S(2)}, u32[]{:S(2)}) %collective-permute-start.56) | collective-permute-done | bytes 544800 | tf_op jit(solution)/shard_map/ppermute | solution.py:111
  1631.0 20.7 %collective-permute-done.52 = bf16[2,224,448]{2,1,0:T(8,128)(2,1)} collective-permute-done((bf16[2,224,448]{2,1,0:T(8,128)(2,1)S(1)}, bf16[2,224,448]{2,1,0:T(8,128)(2,1)}, u32[]{:S(2)}, u32[]{:S(2)}) %collective-permute-start.52) | collective-permute-done | bytes 401440 | tf_op jit(solution)/shard_map/ppermute | solution.py:111
  1666.1 35.6 %collective-permute-done.39 = bf16[2,224,448]{2,1,0:T(8,128)(2,1)S(1)} collective-permute-done((bf16[2,224,448]{2,1,0:T(8,128)(2,1)S(1)}, bf16[2,224,448]{2,1,0:T(8,128)(2,1)S(1)}, u32[]{:S(2)}, u32[]{:S(2)}) %collective-permute-start.39) | collective-permute-done | bytes 401440 | tf_op jit(solution)/shard_map/ppermute | solution.py:111
  1703.6 21.4 %collective-permute-done.53 = bf16[224,448]{1,0:T(8,128)(2,1)S(1)} collective-permute-done((bf16[224,448]{1,0:T(8,128)(2,1)S(1)}, bf16[224,448]{1,0:T(8,128)(2,1)S(1)}, u32[]{:S(2)}, u32[]{:S(2)}) %collective-permute-start.53) | collective-permute-done | bytes 200736 | tf_op jit(solution)/shard_map/ppermute | solution.py:111
  (745 shorter events, 939.2 us)
Async XLA Ops:
  7.2 165.0 %all-gather.5.cloned.1.call-start = ((), (), s32[]{:S(2)}) async-start(), calls=%async_computation.6 | async-start | bytes 10723328 | tf_op jit(solution)/shard_map/all_gather | solution.py:81
  28.3 369.9 %all-gather.7.cloned.1.call-start = ((), (), s32[]{:S(2)}) async-start(), calls=%async_computation.7 | async-start | bytes 14966784 | tf_op jit(solution)/shard_map/all_gather | solution.py:86
  184.0 74.6 %all-to-all-start.1 = ((bf16[16,32,1792]{2,1,0:T(8,128)(2,1)}), bf16[16,32,1792]{2,1,0:T(8,128)(2,1)S(1)}, u32[]{:S(2)}, u32[]{:S(2)}) async-start(bf16[16,32,1792]{2,1,0:T(8,128)(2,1)} %bitcast.468), calls=%async_computation.1 | async-start | bytes 3670016 | tf_op jit(solution)/shard_map/all_to_all | solution.py:70
  187.9 353.4 %all-gather.9.cloned.1.call-start = ((), (), s32[]{:S(2)}) async-start(), calls=%async_computation.8 | async-start | bytes 8773632 | tf_op jit(solution)/shard_map/all_gather | solution.py:81
  274.5 73.2 %collective-permute-start.3 = (bf16[1,512,1792]{2,1,0:T(8,128)(2,1)S(1)}, bf16[1,512,1792]{2,1,0:T(8,128)(2,1)S(1)}, u32[]{:S(2)}, u32[]{:S(2)}) collective-permute-start(bf16[1,512,1792]{2,1,0:T(8,128)(2,1)S(1)} %fusion.168), channel_id=1, source_target_pairs={{0,2},{2,0},{1,3},{3,1},{4,6},{6,4},{5,7},{7,5},{8,10},{10,8},{9,1... | collective-permute-start | bytes 5505032 | tf_op jit(solution)/shard_map/ppermute | solution.py:111
  310.7 90.8 %collective-permute-start.6 = (bf16[2,512,1792]{2,1,0:T(8,128)(2,1)}, bf16[2,512,1792]{2,1,0:T(8,128)(2,1)}, u32[]{:S(2)}, u32[]{:S(2)}) collective-permute-start(bf16[2,512,1792]{2,1,0:T(8,128)(2,1)} %pad_maximum_fusion.7), channel_id=1, source_target_pairs={{0,1},{1,0},{2,3},{3,2},{4,5},{5,4},{6,7},{7,6},{8,9},{9,8},{10,11... | collective-permute-start | bytes 11010056 | tf_op jit(solution)/shard_map/ppermute | solution.py:77
  401.0 346.3 %all-gather.11.cloned.1.call-start = ((), (), s32[]{:S(2)}) async-start(), calls=%async_computation.9 | async-start | bytes 14966784 | tf_op jit(solution)/shard_map/all_gather | solution.py:86
  456.0 97.4 %collective-permute-start.8 = (bf16[512,1792]{1,0:T(8,128)(2,1)}, bf16[512,1792]{1,0:T(8,128)(2,1)}, u32[]{:S(2)}, u32[]{:S(2)}) collective-permute-start(bf16[512,1792]{1,0:T(8,128)(2,1)} %fusion.173), channel_id=1, source_target_pairs={{0,2},{2,0},{1,3},{3,1},{4,6},{6,4},{5,7},{7,5},{8,10},{10,8},{9,1... | collective-permute-start | bytes 5505032 | tf_op jit(solution)/shard_map/ppermute | solution.py:111
  544.6 1202.9 %reduce-scatter.7.cloned.1.call-start = ((), (), s32[]{:S(2)}) async-start(), calls=%async_computation.11 | async-start | bytes 8773632
  1142.5 614.5 %reduce-scatter.5.cloned.1.call-start = ((), (), s32[]{:S(2)}) async-start(), calls=%async_computation.10 | async-start | bytes 14966784 | tf_op jit(solution)/shard_map/reduce_scatter | solution.py:91
  1278.2 144.0 %collective-permute-start.34 = (bf16[896,2432]{1,0:T(8,128)(2,1)}, bf16[896,2432]{1,0:T(8,128)(2,1)}, u32[]{:S(2)}, u32[]{:S(2)}) collective-permute-start(bf16[896,2432]{1,0:T(8,128)(2,1)} %convolution_convert_fusion.2), channel_id=1, source_target_pairs={{0,16},{16,0},{1,17},{17,1},{2,18},{18,2},{3,19},{19,3},{4,20},{20... | collective-permute-start | bytes 13074440 | tf_op jit(solution)/shard_map/ppermute | solution.py:111
  1316.9 105.4 %collective-permute-start.35 = (bf16[2,224,1216]{2,1,0:T(8,128)(2,1)}, bf16[2,224,1216]{2,1,0:T(8,128)(2,1)}, u32[]{:S(2)}, u32[]{:S(2)}) collective-permute-start(bf16[2,224,1216]{2,1,0:T(8,128)(2,1)} %get-tuple-element.197), channel_id=1, source_target_pairs={{0,4},{4,0},{8,12},{12,8},{1,5},{5,1},{9,13},{13,9},{2,6},{6,2},{1... | collective-permute-start | bytes 3268616 | tf_op jit(solution)/shard_map/ppermute | solution.py:111
  1352.3 272.3 %all-to-all-start.2 = ((bf16[16,32,1792]{2,1,0:T(8,128)(2,1)}), bf16[16,32,1792]{2,1,0:T(8,128)(2,1)S(1)}, u32[]{:S(2)}, u32[]{:S(2)}) async-start(bf16[16,32,1792]{2,1,0:T(8,128)(2,1)} %bitcast.466), calls=%async_computation.2 | async-start | bytes 3670016 | tf_op jit(solution)/shard_map/all_to_all | solution.py:70
  1364.5 139.3 %collective-permute-start.50 = (bf16[2,896,448]{1,2,0:T(8,128)(2,1)}, bf16[2,896,448]{1,2,0:T(8,128)(2,1)}, u32[]{:S(2)}, u32[]{:S(2)}) collective-permute-start(bf16[2,896,448]{1,2,0:T(8,128)(2,1)} %fusion.209), channel_id=1, source_target_pairs={{0,16},{16,0},{1,17},{17,1},{2,18},{18,2},{3,19},{19,3},{4,20},{20... | collective-permute-start | bytes 4816904 | tf_op jit(solution)/shard_map/ppermute | solution.py:111
  1399.9 118.8 %collective-permute-start.41 = (bf16[1,1792,448]{1,2,0:T(8,128)(2,1)}, bf16[1,1792,448]{1,2,0:T(8,128)(2,1)}, u32[]{:S(2)}, u32[]{:S(2)}) collective-permute-start(bf16[1,1792,448]{1,2,0:T(8,128)(2,1)} %fusion.124), channel_id=1, source_target_pairs={{0,2},{2,0},{1,3},{3,1},{4,6},{6,4},{5,7},{7,5},{8,10},{10,8},{9,1... | collective-permute-start | bytes 4816904 | tf_op jit(solution)/shard_map/ppermute | solution.py:111
  1425.4 77.3 %collective-permute-start.56 = (bf16[224,1216]{1,0:T(8,128)(2,1)S(1)}, bf16[224,1216]{1,0:T(8,128)(2,1)S(1)}, u32[]{:S(2)}, u32[]{:S(2)}) collective-permute-start(bf16[224,1216]{1,0:T(8,128)(2,1)S(1)} %dynamic-slice_bitcast_fusion.4), channel_id=1, source_target_pairs={{0,8},{4,12},{8,0},{12,4},{1,9},{5,13},{9,1},{13,5},{2,10},{6,14},... | collective-permute-start | bytes 1634312 | tf_op jit(solution)/shard_map/ppermute | solution.py:111
  1453.9 98.0 %collective-permute-start.37 = (bf16[2,896,448]{1,2,0:T(8,128)(2,1)}, bf16[2,896,448]{1,2,0:T(8,128)(2,1)}, u32[]{:S(2)}, u32[]{:S(2)}) collective-permute-start(bf16[2,896,448]{1,2,0:T(8,128)(2,1)} %fusion.206), channel_id=1, source_target_pairs={{0,16},{16,0},{1,17},{17,1},{2,18},{18,2},{3,19},{19,3},{4,20},{20... | collective-permute-start | bytes 4816904 | tf_op jit(solution)/shard_map/ppermute | solution.py:111
  1502.7 107.5 %collective-permute-start.54 = (bf16[2,224,2432]{2,1,0:T(8,128)(2,1)}, bf16[2,224,2432]{2,1,0:T(8,128)(2,1)}, u32[]{:S(2)}, u32[]{:S(2)}) collective-permute-start(bf16[2,224,2432]{2,1,0:T(8,128)(2,1)} %dynamic-slice_bitcast_fusion), channel_id=1, source_target_pairs={{0,4},{4,0},{8,12},{12,8},{1,5},{5,1},{9,13},{13,9},{2,6},{6,2},{1... | collective-permute-start | bytes 6537224 | tf_op jit(solution)/shard_map/ppermute | solution.py:111
  1517.3 99.7 %collective-permute-start.51 = (bf16[4,224,448]{2,1,0:T(8,128)(2,1)}, bf16[4,224,448]{2,1,0:T(8,128)(2,1)}, u32[]{:S(2)}, u32[]{:S(2)}) collective-permute-start(bf16[4,224,448]{2,1,0:T(8,128)(2,1)} %bitcast.519), channel_id=1, source_target_pairs={{0,2},{2,0},{1,3},{3,1},{4,6},{6,4},{5,7},{7,5},{8,10},{10,8},{9,1... | collective-permute-start | bytes 2408456 | tf_op jit(solution)/shard_map/ppermute | solution.py:111
  1549.5 71.1 %collective-permute-start.42 = (bf16[4,224,448]{2,1,0:T(8,128)(2,1)}, bf16[4,224,448]{2,1,0:T(8,128)(2,1)}, u32[]{:S(2)}, u32[]{:S(2)}) collective-permute-start(bf16[4,224,448]{2,1,0:T(8,128)(2,1)} %bitcast.520), channel_id=1, source_target_pairs={{0,16},{16,0},{1,17},{17,1},{2,18},{18,2},{3,19},{19,3},{4,20},{20... | collective-permute-start | bytes 2408456 | tf_op jit(solution)/shard_map/ppermute | solution.py:111
  1614.0 123.1 %collective-permute-start.55 = (bf16[224,2432]{1,0:T(8,128)(2,1)}, bf16[224,2432]{1,0:T(8,128)(2,1)}, u32[]{:S(2)}, u32[]{:S(2)}) collective-permute-start(bf16[224,2432]{1,0:T(8,128)(2,1)} %dynamic-slice_bitcast_fusion.3), channel_id=1, source_target_pairs={{0,8},{4,12},{8,0},{12,4},{1,9},{5,13},{9,1},{13,5},{2,10},{6,14},... | collective-permute-start | bytes 3268616 | tf_op jit(solution)/shard_map/ppermute | solution.py:111
  1624.7 125.9 %all-to-all-start.3 = ((bf16[16,32,1792]{2,1,0:T(8,128)(2,1)}), bf16[16,32,1792]{2,1,0:T(8,128)(2,1)}, u32[]{:S(2)}, u32[]{:S(2)}) async-start(bf16[16,32,1792]{2,1,0:T(8,128)(2,1)} %bitcast.467), calls=%async_computation.3 | async-start | bytes 3670016 | tf_op jit(solution)/shard_map/all_to_all | solution.py:70
  1629.2 72.5 %collective-permute-start.39 = (bf16[2,224,448]{2,1,0:T(8,128)(2,1)S(1)}, bf16[2,224,448]{2,1,0:T(8,128)(2,1)S(1)}, u32[]{:S(2)}, u32[]{:S(2)}) collective-permute-start(bf16[2,224,448]{2,1,0:T(8,128)(2,1)S(1)} %dynamic-slice_bitcast_fusion.7), channel_id=1, source_target_pairs={{0,4},{4,0},{8,12},{12,8},{1,5},{5,1},{9,13},{13,9},{2,6},{6,2},{1... | collective-permute-start | bytes 1204232 | tf_op jit(solution)/shard_map/ppermute | solution.py:111
  1652.9 72.1 %collective-permute-start.53 = (bf16[224,448]{1,0:T(8,128)(2,1)S(1)}, bf16[224,448]{1,0:T(8,128)(2,1)S(1)}, u32[]{:S(2)}, u32[]{:S(2)}) collective-permute-start(bf16[224,448]{1,0:T(8,128)(2,1)S(1)} %dynamic-slice_bitcast_fusion.8), channel_id=1, source_target_pairs={{0,8},{4,12},{8,0},{12,4},{1,9},{5,13},{9,1},{13,5},{2,10},{6,14},... | collective-permute-start | bytes 602120 | tf_op jit(solution)/shard_map/ppermute | solution.py:111
  (205 other events, 4147.7 us)
Sparse Core Ops, SparseCore 0:
  11.3 160.8 all-gather.4
  175.8 222.4 all-gather.6
  401.6 139.6 all-gather.8
  544.7 202.4 all-gather.10
  1142.6 178.0 reduce-scatter.6
  1324.2 321.4 reduce-scatter.4
